TPU v7x, 256 devices: a whole 4x4x8 slice. The times are simulated.
256 devices in a mesh: dp: 16 (over y, z_lo), tensor: 16 (over z_hi, x, core).
Axes of the slice: x: 4, y: 4, z: 8 (z_hi: 2, z_lo: 4; z = z_hi * 4 + z_lo), core: 2. Of those that a mesh axis runs over, the one named last changes fastest.
Arguments:
- inputs: bfloat16 [4096, 2560], P(('dp', 'tensor')), may hold values from -6 to 6
- gate_weight: bfloat16 [2560, 12800], P(None, 'tensor'), may hold values from -0.125 to 0.125
- up_weight: bfloat16 [2560, 12800], P(None, 'tensor'), may hold values from -0.125 to 0.125
- down_weight: bfloat16 [12800, 2560], P('tensor'), may hold values from -0.0546875 to 0.0546875
- gate_adapter_in: bfloat16 [2560, 32], replicated, may hold values from -0.125 to 0.125
- b_gate: bfloat16 [32, 12800], P(None, 'tensor'), may hold values from -0.29882812 to 0.29882812
- upper_adapter_in: bfloat16 [2560, 32], replicated, may hold values from -0.125 to 0.125
- b_up: bfloat16 [32, 12800], P(None, 'tensor'), may hold values from -0.29882812 to 0.29882812
- down_adapter_in: bfloat16 [12800, 32], P('tensor'), may hold values from -0.0546875 to 0.0546875
- b_down: bfloat16 [32, 2560], replicated, may hold values from -0.29882812 to 0.29882812
- m_gate: float32 [12800], P('tensor'), may hold values from 0.5 to 2
- m_up: float32 [12800], P('tensor'), may hold values from 0.5 to 2
- m_down: float32 [2560], replicated, may hold values from 0.5 to 2
- cotangent: bfloat16 [4096, 2560], P(('dp', 'tensor')), may hold values from -6 to 6
Outputs:
- outputs: bfloat16 [4096, 2560], P(('dp', 'tensor'))
- input_gradient: bfloat16 [4096, 2560], P(('dp', 'tensor'))
- gate_adapter_in_gradient: float32 [2560, 32], P(('dp', 'tensor'))
- upper_adapter_in_gradient: float32 [2560, 32], P(('dp', 'tensor'))
- gate_adapter_out_gradient: float32 [32, 12800], P(None, 'tensor')
- upper_adapter_out_gradient: float32 [32, 12800], P(None, 'tensor')
- down_adapter_in_gradient: float32 [12800, 32], P('tensor')
- down_adapter_out_gradient: float32 [32, 2560], P(None, ('dp', 'tensor'))
- grad_m_gate: float32 [12800], P('tensor')
- grad_m_up: float32 [12800], P('tensor')
- grad_m_down: float32 [2560], P(('dp', 'tensor'))
All inputs are finite; a program needn't handle non-finite values.
Results may differ from a plain program's by a relative error of at most 0.024.
Values may be sent and summed in bfloat16 or wider, within the bound.
No kernel may reach another device: no remote copies, remote signals or barrier semaphores. Data moves between devices by JAX's collectives and lax.ppermute only.
A program may use at most 128 MiB of HBM per device.

v0:
```python
import jax
import jax.numpy as jnp
from jax import lax
from jax.experimental import pallas as pl
from jax.experimental.pallas import tpu as pltpu
from jax.sharding import Mesh, PartitionSpec as P

adapter_scale = 2.0
epsilon = 1e-06
bf16 = jnp.bfloat16
f32 = jnp.float32

DATA = ("y", "zl")
TENSOR = ("zh", "x", "c")
ALL = DATA + TENSOR
X_ORDER = (1, 3, 2)
MIB = 1024 * 1024
ANY = pl.BlockSpec(memory_space=pl.ANY)
VMEM = pl.BlockSpec(memory_space=pltpu.VMEM)
SMEM = pl.BlockSpec(memory_space=pltpu.SMEM)
SPANS = ((0, 256), (256, 256), (512, 288))
WIDE = 640
RANK = 32
SHARED = 64


def swap(value, axis, distance, size):
    return lax.ppermute(value, axis, [(i, i ^ distance) for i in range(size)])


def swap_core(value):
    return swap(value, "c", 1, 2)


def swap_z(value):
    return swap(value, ("zl", "zh"), 5, 8)


def swap_x(value):
    return [swap(value, "x", k, 4) for k in X_ORDER]


def dot(a, b):
    return jnp.dot(a, b, preferred_element_type=f32)


def dot_last(a, b):
    return lax.dot_general(a, b, (((1,), (1,)), ((), ())), preferred_element_type=f32)


def dot_first(a, b):
    return lax.dot_general(a, b, (((0,), (0,)), ((), ())), preferred_element_type=f32)


def shape(*dims, dtype=bf16):
    return jax.ShapeDtypeStruct(dims, dtype)


def call(kernel, name, out_shape, mib, flops=1000, **kwargs):
    return pl.pallas_call(
        kernel,
        out_shape=out_shape,
        compiler_params=pltpu.CompilerParams(vmem_limit_bytes=mib * MIB),
        cost_estimate=pl.CostEstimate(flops=flops, bytes_accessed=1000, transcendentals=0),
        name=name,
        **kwargs,
    )


def parts(features):
    return [pl.ds(i, WIDE) for i in range(0, features, WIDE)]


def down_squares_kernel(w_ref, a_ref, b_ref, squares_ref):
    for part in parts(w_ref.shape[1]):
        merged = w_ref[:, part].astype(f32) + adapter_scale * dot_first(a_ref[...], b_ref[:, part])
        squares_ref[:, part] = jnp.sum(merged * merged, axis=0, keepdims=True)


def down_squares(weight, left_t, right):
    return call(
        down_squares_kernel,
        "down_squares",
        shape(1, weight.shape[1], dtype=f32),
        6,
        in_specs=[VMEM] * 3,
        out_specs=VMEM,
    )(weight, left_t, right)


class Copies:
    def __init__(self, pairs, sems, ahead):
        self.copies = [pltpu.make_async_copy(a, b, sems.at[i]) for i, (a, b) in enumerate(pairs)]
        self.started = self.waited = 0
        self.ahead = ahead
        self.fill()

    def fill(self):
        while self.started < min(len(self.copies), self.waited + self.ahead):
            self.copies[self.started].start()
            self.started += 1

    def wait(self):
        self.copies[self.waited].wait()
        self.waited += 1
        self.fill()


def merge_kernel(
    after, g_ref, u_ref, d_ref, ga, ua, gb, ub, ad, bd, g_m, u_m, g_out, u_out, d_out, g_scale, u_scale,
    g_held, u_held, d_held, sems,
):
    spans = parts(g_ref.shape[1])
    pairs = []
    for ref, held in ((g_ref, g_held), (u_ref, u_held), (d_ref, d_held)):
        pairs += [(ref.at[:, part], held.at[:, part]) for part in spans]
    copies = Copies(pairs, sems, 6)
    for w, a, b, m, out, scale in ((g_held, ga, gb, g_m, g_out, g_scale), (u_held, ua, ub, u_m, u_out, u_scale)):
        squares = 0.0
        for part in spans:
            copies.wait()
            merged = w[:, part].astype(f32) + adapter_scale * dot_first(b[...], a[:, part])
            out[:, part] = merged.astype(bf16)
            square = merged * merged
            squares += sum(square[:, k : k + 128] for k in range(0, WIDE, 128))
        total = jnp.sum(jnp.transpose(squares), axis=0, keepdims=True)
        scale[...] = m[...] / jnp.sqrt(total + epsilon)
    for part in spans:
        copies.wait()
        merged = d_held[:, part].astype(f32) + adapter_scale * dot_first(ad[...], bd[:, part])
        d_out[:, part] = merged.astype(bf16)


def merge(after, gate, up, down, *others):
    units, features = gate.shape
    return call(
        merge_kernel,
        "merge",
        [shape(*gate.shape)] * 3 + [shape(1, units, dtype=f32)] * 2,
        40,
        in_specs=[ANY] * 4 + [VMEM] * len(others),
        out_specs=[VMEM] * 5,
        scratch_shapes=[pltpu.VMEM(gate.shape, bf16)] * 3 + [pltpu.SemaphoreType.DMA((3 * (features // WIDE),))],
    )(after, gate, up, down, *others)


def forward_kernel(
    after, mine, away, gate, up, down, ga_t, ua_t, ad_t, g_scale, u_scale,
    p_mine, p_away, hidden_out, gate_out, up_out, rank_in_t, rank_down_t, rows,
):
    half = mine.shape[0]
    rows[:half] = mine[...]
    rows[half:] = away[...]
    rank_down = 0.0
    for start, size in SPANS:
        span = pl.ds(start, size)
        gate_value = dot_last(rows[...], gate[span, :]) * g_scale[:, span]
        up_value = dot_last(rows[...], up[span, :]) * u_scale[:, span]
        gate_out[:, span] = gate_value.astype(bf16)
        up_out[:, span] = up_value.astype(bf16)
        hidden = (gate_value * jax.nn.sigmoid(gate_value) * up_value).astype(bf16)
        hidden_out[:, span] = hidden
        rank_down += dot_last(ad_t[:, span], hidden)
    rank_down_t[...] = rank_down.astype(bf16)
    for part in parts(down.shape[1]):
        p = dot(hidden_out[...], down[:, part]).astype(bf16)
        p_mine[:, part] = p[:half]
        p_away[:, part] = p[half:]
    rank_in_t[:RANK, :] = dot_last(ga_t[...], rows[...]).astype(bf16)
    rank_in_t[RANK:, :] = dot_last(ua_t[...], rows[...]).astype(bf16)


def forward(after, mine, *others):
    half, features = mine.shape
    units = others[1].shape[0]
    return call(
        forward_kernel,
        "forward",
        [shape(half, features)] * 2 + [shape(2 * half, units)] * 3 + [shape(2 * RANK, 2 * half), shape(RANK, 2 * half)],
        6,
        in_specs=[ANY] + [VMEM] * (1 + len(others)),
        out_specs=[VMEM] * 7,
        scratch_shapes=[pltpu.VMEM((2 * half, features), bf16)],
    )(after, mine, *others)


def backward_kernel(
    y, core, cot_mine, cot_away, mine, away, p_mine, p_away, down, hidden, gate_value, up_value,
    rank_in_t, rank_down_t, b_down, b_gate, b_up, g_scale, u_scale, m_gate, m_up, d_sq, m_down,
    delta_gate_out, delta_up_out, shared_own, shared_away, local_out,
    delta, local,
):
    units, features = down.shape
    half = mine.shape[0]
    block = features // 4
    norm_down = jnp.sqrt(d_sq[...] + epsilon)
    scale_down = m_down[...] / norm_down
    delta[:half] = (cot_mine[...].astype(f32) * scale_down).astype(bf16)
    delta[half:] = (cot_away[...].astype(f32) * scale_down).astype(bf16)
    back_down_t = dot_last(b_down[...], delta[...]).astype(bf16)
    back_gate = back_up = 0.0
    local[:, :, pl.ds(768, 512)] = jnp.zeros((4, RANK, 512), bf16)
    for start, size in SPANS:
        span = pl.ds(start, size)
        grad_hidden = dot_last(delta[...], down[span, :])
        gate = gate_value[:, span].astype(f32)
        upper = up_value[:, span].astype(f32)
        logistic = jax.nn.sigmoid(gate)
        activated = gate * logistic
        grad_up = grad_hidden * activated
        grad_gate = grad_hidden * upper * (logistic + activated * (1.0 - logistic))
        grad_m_gate = jnp.sum(grad_gate * gate, axis=0, keepdims=True) / m_gate[:, span]
        grad_m_up = jnp.sum(grad_up * upper, axis=0, keepdims=True) / m_up[:, span]
        delta_gate = (grad_gate * g_scale[:, span]).astype(bf16)
        delta_up = (grad_up * u_scale[:, span]).astype(bf16)
        delta_gate_out[:, span] = delta_gate
        delta_up_out[:, span] = delta_up
        back_gate += dot_last(b_gate[:, span], delta_gate)
        back_up += dot_last(b_up[:, span], delta_up)
        local[0, :, span] = (adapter_scale * dot(rank_in_t[:RANK, :], delta_gate)).astype(bf16)
        local[1, :, span] = (adapter_scale * dot(rank_in_t[RANK:, :], delta_up)).astype(bf16)
        local[2, :, span] = (adapter_scale * dot(back_down_t, hidden[:, span])).astype(bf16)
        stats = jnp.concatenate([grad_m_gate, grad_m_up, jnp.zeros((RANK - 2, size), f32)], axis=0)
        local[3, :, span] = stats.astype(bf16)
    back_t = jnp.concatenate([back_gate, back_up], axis=0).astype(bf16)
    here = y[0]
    first = core[0] == 0
    for k in range(4):
        chunk = here ^ k
        part = pl.ds(pl.multiple_of(chunk * block, 128), block)
        own = local[chunk]
        folded = sum(
            pltpu.roll(own[i * 8 : (i + 1) * 8, block:].astype(f32), i * (units - block), 1) for i in range(4)
        )
        local_out[k, pl.ds(0, RANK), :] = own[:, :block]
        folded = jnp.concatenate([folded, jnp.zeros((8, block), f32)], axis=0)
        local_out[k, pl.ds(RANK, 16), :] = folded.astype(bf16)
        back_rows = adapter_scale * (dot(back_t[:, :half], mine[:, part]) + dot(back_t[:, half:], away[:, part]))
        down_rows = adapter_scale * dot(rank_down_t[...], delta[:, part])
        moment = sum(
            jnp.sum(cot[:, part].astype(f32) * partial[:, part].astype(f32), axis=0, keepdims=True)
            for cot, partial in ((cot_mine, p_mine), (cot_away, p_away))
        )
        moment = moment / jnp.sqrt(d_sq[:, part] + epsilon)
        zeros = jnp.zeros((15, block), f32)
        one = jnp.concatenate([back_rows[:RANK], down_rows[:16], jnp.zeros((16, block), f32)], axis=0)
        two = jnp.concatenate([back_rows[RANK:], down_rows[16:], moment, zeros], axis=0)
        shared_own[k] = jnp.where(first, one, two).astype(bf16)
        shared_away[k] = jnp.where(first, two, one).astype(bf16)


def backward(y, core, *others):
    half, features = others[0].shape
    units = others[6].shape[0]
    return call(
        backward_kernel,
        "backward",
        [shape(2 * half, units)] * 2 + [shape(4, SHARED, features // 4)] * 2 + [shape(4, RANK + 16, features // 4)],
        10,
        in_specs=[SMEM] * 2 + [VMEM] * len(others),
        out_specs=[VMEM] * 5,
        scratch_shapes=[pltpu.VMEM((2 * half, features), bf16), pltpu.VMEM((4, RANK, 2 * (features // 4)), bf16)],
    )(y, core, *others)


def input_gradient_kernel(delta_gate, delta_up, gate, up, mine, away):
    half = mine.shape[0]
    for part in parts(gate.shape[1]):
        total = dot(delta_gate[...], gate[:, part]) + dot(delta_up[...], up[:, part])
        total = total.astype(bf16)
        mine[:, part] = total[:half]
        away[:, part] = total[half:]


def input_gradient_of(delta_gate, delta_up, gate, up):
    rows = delta_gate.shape[0] // 2
    return call(
        input_gradient_kernel,
        "input_gradient",
        [shape(rows, gate.shape[1])] * 2,
        5,
        flops=8 * rows * gate.size,
        in_specs=[VMEM] * 4,
        out_specs=[VMEM, VMEM],
    )(delta_gate, delta_up, gate, up)


def core_sum_kernel(after, own, got, local, out0, out1, out2, out3):
    for k, out in enumerate((out0, out1, out2, out3)):
        total = own[k].astype(f32) + got[k].astype(f32)
        folded = local[k, pl.ds(RANK, 16), :].astype(f32)
        out[pl.ds(0, SHARED), :] = jnp.concatenate([total[: SHARED - 8], folded[:8]], axis=0).astype(bf16)
        out[pl.ds(SHARED, RANK), :] = local[k, pl.ds(0, RANK), :]


def core_sum(after, own, got, local):
    return call(
        core_sum_kernel,
        "core_sum",
        [shape(SHARED + RANK, own.shape[2])] * 4,
        4,
        in_specs=[ANY] + [VMEM] * 3,
        out_specs=[VMEM] * 4,
    )(after, own, got, local)


def after_y_kernel(zl, after, own, a, b, c, out0, out1, out2, out3, shared):
    total = own[...].astype(f32) + a[...].astype(f32) + b[...].astype(f32) + c[...].astype(f32)
    wide = out0.shape[1]
    quarter = total.shape[1] // 4
    here = zl[0]
    for j in range(4):
        shared[j, :, pl.ds(0, quarter)] = total[:SHARED, j * quarter : (j + 1) * quarter]
    folded = total[SHARED - 8 : SHARED]
    rest = jnp.concatenate([folded[:, i * quarter : (i + 1) * quarter] for i in range(4)], axis=0)
    local = jnp.concatenate([total[SHARED:], rest], axis=1).astype(bf16)
    for k, out in enumerate((out0, out1, out2, out3)):
        out[pl.ds(0, SHARED), :] = shared[here ^ k].astype(bf16)
        for i in range(3):
            out[pl.ds(SHARED + i * RANK, RANK), :] = local[:, i * wide : (i + 1) * wide]
        out[pl.ds(SHARED + 3 * RANK, RANK), pl.ds(0, local.shape[1] - 3 * wide)] = local[:, 3 * wide :]


def after_y(zl, after, own, others):
    return call(
        after_y_kernel,
        "after_y",
        [shape(SHARED + 4 * RANK, 256)] * 4,
        4,
        in_specs=[SMEM, ANY] + [VMEM] * 4,
        out_specs=[VMEM] * 4,
        scratch_shapes=[pltpu.VMEM((4, SHARED, 256), f32)],
    )(zl, after, own, *others)


def after_z_kernel(own, a, b, c, shared, local):
    total = own[...].astype(f32) + a[...].astype(f32) + b[...].astype(f32) + c[...].astype(f32)
    shared[...] = total[:SHARED, : shared.shape[1]]
    wide = own.shape[1]
    for i in range(4):
        width = min(wide, local.shape[1] - i * wide)
        first = SHARED + i * RANK
        local[:, pl.ds(i * wide, width)] = total[first : first + RANK, :width].astype(bf16)


def after_z(own, others, quarter, units):
    return call(
        after_z_kernel,
        "after_z",
        [shape(SHARED, quarter, dtype=f32), shape(RANK, units)],
        4,
        in_specs=[VMEM] * 4,
        out_specs=[VMEM] * 2,
    )(own, *others)


def x_sum_kernel(own, a, b, c, local, out, sent, local_out):
    total = own[...] + a[...].astype(f32) + b[...].astype(f32) + c[...].astype(f32)
    out[...] = total
    sent[...] = total.astype(bf16)
    local_out[...] = local[...]


def x_sum(own, others, local):
    return call(
        x_sum_kernel,
        "x_sum",
        [shape(*own.shape, dtype=f32), shape(*own.shape), shape(*local.shape)],
        4,
        in_specs=[VMEM] * 5,
        out_specs=[VMEM] * 3,
    )(own, *others, local)


def local_out_kernel(y, own, a, b, c, gate, up, down, stats, held):
    for k, piece in enumerate((own, a, b, c)):
        held[k] = piece[...]
    here = y[0]
    for j, out in enumerate((gate, up, down)):
        out[...] = held[here ^ j].astype(f32)
    stats[...] = held[here ^ 3][:8].astype(f32)


def local_out(y, own, others):
    units = own.shape[1]
    return call(
        local_out_kernel,
        "local_out",
        [shape(RANK, units, dtype=f32)] * 3 + [shape(8, units, dtype=f32)],
        4,
        in_specs=[SMEM] + [VMEM] * 4,
        out_specs=[VMEM] * 4,
        scratch_shapes=[pltpu.VMEM((4, RANK, units), bf16)],
    )(y, own, *others)


def shared_out_kernel(place, core, own, got, gate, up, down, moment):
    wide = gate.shape[0]
    first = core[0] == 0
    halves = jnp.where(first, own[...], got[...]), jnp.where(first, got[...], own[...])
    spots = (16, own.shape[1])
    row = lax.broadcasted_iota(jnp.int32, spots, 0)
    chosen = (lax.broadcasted_iota(jnp.int32, spots, 1) == place[0] * wide + row).astype(f32)
    highest = lax.Precision.HIGHEST
    last = (((1,), (1,)), ((), ()))
    one, two = [lax.dot_general(chosen, h, last, precision=highest, preferred_element_type=f32) for h in halves]
    gate[...] = one[:wide, :RANK]
    up[...] = two[:wide, :RANK]
    down[:, pl.ds(0, 16)] = one[:wide, RANK : RANK + 16]
    down[:, pl.ds(16, 16)] = two[:wide, RANK : RANK + 16]
    line = lax.dot_general(halves[1][48:56], chosen, last, precision=highest, preferred_element_type=f32)
    moment[...] = line[:1, :wide]


def shared_out(place, core, own, got):
    wide = own.shape[1] // 16
    return call(
        shared_out_kernel,
        "shared_out",
        [shape(wide, RANK, dtype=f32)] * 3 + [shape(1, wide, dtype=f32)],
        4,
        in_specs=[SMEM] * 2 + [VMEM] * 2,
        out_specs=[VMEM] * 4,
    )(place, core, own, got)


def half_sum_kernel(p_mine, p_got, i_mine, i_got, pair, one, two, three):
    part = p_mine.shape[0] // 4
    for place, mine, got in ((0, p_mine, p_got), (part, i_mine, i_got)):
        rows = pl.ds(place, part)
        total = mine[...].astype(f32) + got[...].astype(f32)
        pair[rows, :] = total[:part]
        for i, out in enumerate((one, two, three)):
            out[rows, :] = total[(i + 1) * part : (i + 2) * part].astype(bf16)


def half_sum(p_mine, p_got, i_mine, i_got):
    rows, features = p_mine.shape
    part = rows // 2
    return call(
        half_sum_kernel,
        "half_sum",
        [shape(part, features, dtype=f32)] + [shape(part, features)] * 3,
        5,
        in_specs=[VMEM] * 4,
        out_specs=[VMEM] * 4,
    )(p_mine, p_got, i_mine, i_got)


def pair_sum_kernel(pair, a, b, c, own, sent):
    total = pair[...] + a[...].astype(f32) + b[...].astype(f32) + c[...].astype(f32)
    rows = total.shape[0] // 4
    for i in range(2):
        first = 2 * i * rows
        own[pl.ds(i * rows, rows), :] = total[first : first + rows]
        sent[pl.ds(i * rows, rows), :] = total[first + rows : first + 2 * rows].astype(bf16)


def pair_sum(pair, got):
    rows, features = pair.shape
    return call(
        pair_sum_kernel,
        "pair_sum",
        [shape(rows // 2, features, dtype=f32), shape(rows // 2, features)],
        4,
        in_specs=[VMEM] * 4,
        out_specs=[VMEM] * 2,
    )(pair, *got)


def rows_out_kernel(own, got, d_sq, m_down, outputs, input_gradient):
    rows = outputs.shape[0]
    total = own[...] + got[...].astype(f32)
    scale_down = m_down[...] / jnp.sqrt(d_sq[...] + epsilon)
    outputs[...] = (total[:rows] * scale_down).astype(bf16)
    input_gradient[...] = total[rows:].astype(bf16)


def rows_out(own, got, d_sq, m_down):
    rows, features = own.shape
    return call(
        rows_out_kernel,
        "rows_out",
        [shape(rows // 2, features)] * 2,
        4,
        in_specs=[VMEM] * 4,
        out_specs=[VMEM] * 2,
    )(own, got, d_sq, m_down)


def held_until_kernel(after, value, out):
    out[...] = value[...]


def held_until(after, value):
    return call(
        held_until_kernel,
        "held_until",
        shape(*value.shape, dtype=value.dtype),
        2,
        in_specs=[ANY, VMEM],
        out_specs=VMEM,
    )(after, value)


def split(value):
    high = value.astype(bf16)
    return jnp.concatenate([high, (value - high.astype(f32)).astype(bf16)], axis=0)


def joined(rows):
    return rows[0:1].astype(f32) + rows[1:2].astype(f32)


def shards(
    inputs, gate_weight, up_weight, down_weight, gate_adapter_in, b_gate, upper_adapter_in, b_up,
    down_adapter_in, b_down, m_gate, m_up, m_down, cotangent,
):
    rows, features = inputs.shape
    units = down_weight.shape[0]
    y, zl, core = lax.axis_index("y")[None], lax.axis_index("zl")[None], lax.axis_index("c")[None]
    place = (lax.axis_index("zh") * 4 + lax.axis_index("x")) * 2 + lax.axis_index("c")
    m_gate, m_up, m_down = m_gate[None], m_up[None], m_down[None]
    gate_t, up_t = gate_weight.T, up_weight.T
    ga_t, ua_t, ad_t = gate_adapter_in.T, upper_adapter_in.T, down_adapter_in.T

    other = swap_z(inputs)
    squares = held_until(other, down_squares(down_weight, ad_t, b_down))
    got = swap_z(jnp.concatenate([cotangent, split(squares)], axis=0))
    pair = jnp.concatenate([inputs, other], axis=0)
    got_x = swap_x(pair)
    mine = jnp.concatenate([pair] + got_x, axis=0)
    squares = squares + joined(got[rows:])
    pair = jnp.concatenate([cotangent, got[:rows]], axis=0)
    got = swap_x(jnp.concatenate([pair, split(squares)], axis=0))

    gate, up, down, g_scale, u_scale = merge(
        got_x[0], gate_t, up_t, down_weight, ga_t, ua_t, b_gate, b_up, ad_t, b_down, m_gate, m_up
    )
    away = swap_core(mine)
    cot_mine = jnp.concatenate([pair] + [g[: 2 * rows] for g in got], axis=0)
    cot_away = swap_core(cot_mine)
    squares = squares + sum(joined(g[2 * rows :]) for g in got)
    squares = squares + swap_core(squares)

    p_mine, p_away, hidden, gate_value, up_value, rank_in_t, rank_down_t = forward(
        cot_mine, mine, away, gate, up, down, ga_t, ua_t, ad_t, g_scale, u_scale
    )
    p_got = swap_core(p_away)

    delta_gate, delta_up, shared_own, shared_away, local = backward(
        y, core, cot_mine, cot_away, mine, away, p_mine, p_away, down, hidden, gate_value, up_value,
        rank_in_t, rank_down_t, b_down, b_gate, b_up, g_scale, u_scale, m_gate, m_up, squares, m_down,
    )
    i_mine, i_away = input_gradient_of(delta_gate, delta_up, gate, up)
    packed = core_sum(i_mine, shared_own, swap_core(shared_away), local)
    pair, *sent = half_sum(p_mine, p_got, i_mine, swap_core(i_away))
    own, *sent_z = after_y(zl, pair, packed[0], [swap(packed[k], "y", k, 4) for k in (1, 2, 3)])

    quarter = features // 16
    shared, local = after_z(own, [swap(v, "zl", k + 1, 4) for k, v in enumerate(sent_z)], quarter, units)
    shared, sent_zh, local = x_sum(shared, swap_x(shared.astype(bf16)), local)
    shared = shared + swap(sent_zh, "zh", 1, 2).astype(f32)
    gate_in, up_in, down_in, moment = shared_out(place[None], core, shared, swap_core(shared))
    gate_out, up_out, down_out, stats = local_out(y, local, [swap(local, "y", k, 4) for k in (1, 2, 3)])

    own, sent = pair_sum(pair, [swap(v, "x", k, 4) for k, v in zip(X_ORDER, sent)])
    outputs, input_gradient = rows_out(own, swap_z(sent), squares, m_down)

    return (
        outputs,
        input_gradient,
        gate_in,
        up_in,
        gate_out,
        up_out,
        down_out.T,
        down_in.T,
        stats[0],
        stats[1],
        moment[0],
    )


def solution(mesh):
    fine = Mesh(mesh.devices.reshape(4, 4, 2, 4, 2), ALL)
    return jax.shard_map(
        shards,
        mesh=fine,
        in_specs=(
            P(ALL, None),
            P(None, TENSOR),
            P(None, TENSOR),
            P(TENSOR, None),
            P(),
            P(None, TENSOR),
            P(),
            P(None, TENSOR),
            P(TENSOR, None),
            P(),
            P(TENSOR),
            P(TENSOR),
            P(),
            P(ALL, None),
        ),
        out_specs=(
            P(ALL, None),
            P(ALL, None),
            P(ALL, None),
            P(ALL, None),
            P(None, TENSOR),
            P(None, TENSOR),
            P(TENSOR, None),
            P(None, ALL),
            P(TENSOR),
            P(TENSOR),
            P(ALL),
        ),
        check_vma=False,
    )
```

profile of v0, /device:TPU:32, one launch (start us, length us, event | category | flops | bytes accessed | tf_op | source)
XLA Modules:
  0.0 114.1 jit_solution(10015512293772571645)
XLA Ops:
  0.7 5.5 %collective-permute-start = (bf16[16,2560]{1,0:T(8,128)(2,1)}, bf16[16,2560]{1,0:T(8,128)(2,1)S(1)}, u32[]{:S(2)}, u32[]{:S(2)}) collective-permute-start(bf16[16,2560]{1,0:T(8,128)(2,1)} %param.14), channel_id=1, source_target_pairs={{0,40},{8,32},{16,56},{24,48},{32,8},{40,0},{48,24},{56,16},{1,41}... | collective-permute-start | bytes 245768 | tf_op jit(solution)/shard_map/ppermute | solution.py:28
  6.2 0.9 constant_dynamic-update-slice_fusion.3
  7.1 0.9 constant_dynamic-update-slice_fusion.1
  8.0 2.2 %copy-done = bf16[800,2560]{1,0:T(8,128)(2,1)S(1)} copy-done((bf16[800,2560]{1,0:T(8,128)(2,1)S(1)}, bf16[800,2560]{1,0:T(8,128)(2,1)}, u32[]{:S(2)}) %copy-start) | copy-done | bytes 4096024
  10.2 0.9 copy-done.1
  11.1 0.8 copy-done.5
  11.9 1.6 %down_squares.1.value = f32[1,2560]{1,0:T(1,128)S(1)} custom-call(bf16[800,2560]{1,0:T(8,128)(2,1)S(1)} %copy-done, bf16[32,800]{1,0:T(8,128)(2,1)S(1)} %bitcast.16, bf16[32,2560]{1,0:T(8,128)(2,1)S(1)} %copy-done.1), custom_call_target="tpu_custom_call" | custom-call | flops 1000 | bytes 1000 | tf_op jit(solution)/shard_map/down_squares/pallas_call | solution.py:81
  13.8 1.6 %collective-permute-start.5 = (bf16[32,2560]{1,0:T(8,128)(2,1)S(1)}, bf16[32,2560]{1,0:T(8,128)(2,1)S(1)}, u32[]{:S(2)}, u32[]{:S(2)}) collective-permute-start(bf16[32,2560]{1,0:T(8,128)(2,1)S(1)} %get-tuple-element.113), channel_id=1, source_target_pairs={{0,2},{2,0},{4,6},{6,4},{1,3},{3,1},{5,7},{7,5},{8,10},{10,8},{12,... | collective-permute-start | bytes 491528 | tf_op jit(solution)/shard_map/ppermute | solution.py:28
  15.3 2.1 %collective-permute-start.6 = (bf16[32,2560]{1,0:T(8,128)(2,1)S(1)}, bf16[32,2560]{1,0:T(8,128)(2,1)S(1)}, u32[]{:S(2)}, u32[]{:S(2)}) collective-permute-start(bf16[32,2560]{1,0:T(8,128)(2,1)S(1)} %get-tuple-element.113), channel_id=1, source_target_pairs={{0,6},{2,4},{4,2},{6,0},{1,7},{3,5},{5,3},{7,1},{8,14},{10,12},{12... | collective-permute-start | bytes 491528 | tf_op jit(solution)/shard_map/ppermute | solution.py:28
  17.4 0.6 collective-permute-start.7
  18.1 5.1 %collective-permute-done.1 = bf16[18,2560]{1,0:T(8,128)(2,1)S(1)} collective-permute-done((bf16[18,2560]{1,0:T(8,128)(2,1)S(1)}, bf16[18,2560]{1,0:T(8,128)(2,1)S(1)}, u32[]{:S(2)}, u32[]{:S(2)}) %collective-permute-start.1) | collective-permute-done | bytes 92192 | tf_op jit(solution)/shard_map/ppermute | solution.py:28
  23.3 1.6 %collective-permute-start.2 = (bf16[34,2560]{1,0:T(8,128)(2,1)S(1)}, bf16[34,2560]{1,0:T(8,128)(2,1)S(1)}, u32[]{:S(2)}, u32[]{:S(2)}) collective-permute-start(bf16[34,2560]{1,0:T(8,128)(2,1)S(1)} %pad_maximum_fusion), channel_id=1, source_target_pairs={{0,2},{2,0},{4,6},{6,4},{1,3},{3,1},{5,7},{7,5},{8,10},{10,8},{12,... | collective-permute-start | bytes 522248 | tf_op jit(solution)/shard_map/ppermute | solution.py:28
  24.9 2.1 %collective-permute-start.3 = (bf16[34,2560]{1,0:T(8,128)(2,1)S(1)}, bf16[34,2560]{1,0:T(8,128)(2,1)S(1)}, u32[]{:S(2)}, u32[]{:S(2)}) collective-permute-start(bf16[34,2560]{1,0:T(8,128)(2,1)S(1)} %pad_maximum_fusion), channel_id=1, source_target_pairs={{0,6},{2,4},{4,2},{6,0},{1,7},{3,5},{5,3},{7,1},{8,14},{10,12},{12... | collective-permute-start | bytes 522248 | tf_op jit(solution)/shard_map/ppermute | solution.py:28
  27.0 0.6 collective-permute-start.4
  27.8 3.4 %collective-permute-done.2 = bf16[34,2560]{1,0:T(8,128)(2,1)S(1)} collective-permute-done((bf16[34,2560]{1,0:T(8,128)(2,1)S(1)}, bf16[34,2560]{1,0:T(8,128)(2,1)S(1)}, u32[]{:S(2)}, u32[]{:S(2)}) %collective-permute-start.2) | collective-permute-done | bytes 174112 | tf_op jit(solution)/shard_map/ppermute | solution.py:28
  31.3 5.5 %collective-permute-done.3 = bf16[34,2560]{1,0:T(8,128)(2,1)S(1)} collective-permute-done((bf16[34,2560]{1,0:T(8,128)(2,1)S(1)}, bf16[34,2560]{1,0:T(8,128)(2,1)S(1)}, u32[]{:S(2)}, u32[]{:S(2)}) %collective-permute-start.3) | collective-permute-done | bytes 174112 | tf_op jit(solution)/shard_map/ppermute | solution.py:28
  36.9 0.8 collective-permute-start.11
  37.8 8.0 %merge.1 = (bf16[800,2560]{1,0:T(8,128)(2,1)S(1)}, bf16[800,2560]{1,0:T(8,128)(2,1)S(1)}, bf16[800,2560]{1,0:T(8,128)(2,1)S(1)}, f32[1,800]{1,0:T(1,128)S(1)}, f32[1,800]{1,0:T(1,128)S(1)}) custom-call(bf16[32,2560]{1,0:T(8,128)(2,1)S(1)} %collective-permute-done.5.after, bf16[800,2560]{1,0:T(8,128)(2,1)} %bitcast.19, bf16[800,2560]{1,0:T(8,128)(2,1)} %bitcast.20, ...), custom_call_target="tpu_custom_call" | custom-call | flops 1000 | bytes 1000 | tf_op jit(solution)/shard_map/merge/pallas_call | solution.py:136
  45.8 5.4 %forward.1 = (bf16[128,2560]{1,0:T(8,128)(2,1)S(1)}, bf16[128,2560]{1,0:T(8,128)(2,1)S(1)}, bf16[256,800]{1,0:T(8,128)(2,1)S(1)}, bf16[256,800]{1,0:T(8,128)(2,1...) custom-call(bf16[128,2560]{1,0:T(8,128)(2,1)S(1)} %slice_dynamic-update-slice_fusion.a, ...), custom_call_target="tpu_custom_call" | custom-call | flops 1000 | bytes 1000 | tf_op jit(solution)/shard_map/forward/pallas_call | solution.py:176
  51.5 4.0 %backward.1 = (bf16[256,800]{1,0:T(8,128)(2,1)S(1)}, bf16[256,800]{1,0:T(8,128)(2,1)S(1)}, bf16[4,64,640]{2,1,0:T(8,128)(2,1)S(1)}, bf16[4,64,640]{2,1,0:T(8,128)(2,1)S(1)}, bf16[4,48,640]{2,1,0:T(8,128)(2,1)S(1)}) custom-call(s32[1]{0:T(128)} %bitcast.5.y, s32[1]{0:T(128)} %bitcast.6.core, ...), custom_call_target="tpu_custom_call" | custom-call | flops 1000 | bytes 1000 | tf_op jit(solution)/shard_map/backward/pallas_call | solution.py:255
  55.6 3.3 %input_gradient.1 = (bf16[128,2560]{1,0:T(8,128)(2,1)S(1)}, bf16[128,2560]{1,0:T(8,128)(2,1)S(1)}) custom-call(bf16[256,800]{1,0:T(8,128)(2,1)S(1)} %get-tuple-element.71.delta_gate, bf16[256,800]{1,0:T(8,128)(2,1)S(1)} %get-tuple-element.72.delta_up, bf16[800,2560]{1,0:T(8,128)(2,1)S(1)} %get-tuple-element.59.gate, bf16[800,2560]{1,0:T(8,128)(2,1)S(1)} %get-tuple-element.60.up), custom_call_target="tpu_custom_call" | custom-call | flops 2097152000 | bytes 1000 | tf_op jit(solution)/shard_map/input_gradient/pallas_call | solution.py:277
  58.9 0.5 collective-permute-start.12
  59.5 2.1 %collective-permute-done.17.got = bf16[4,64,640]{2,1,0:T(8,128)(2,1)S(1)} collective-permute-done((bf16[4,64,640]{2,1,0:T(8,128)(2,1)S(1)}, bf16[4,64,640]{2,1,0:T(8,128)(2,1)S(1)}, u32[]{:S(2)}, u32[]{:S(2)}) %collective-permute-start.17) | collective-permute-done | bytes 327712 | tf_op jit(solution)/shard_map/ppermute | solution.py:28
  61.7 1.7 %collective-permute-start.18 = (bf16[96,640]{1,0:T(8,128)(2,1)S(1)}, bf16[96,640]{1,0:T(8,128)(2,1)S(1)}, u32[]{:S(2)}, u32[]{:S(2)}) collective-permute-start(bf16[96,640]{1,0:T(8,128)(2,1)S(1)} %get-tuple-element.87), channel_id=1, source_target_pairs={{0,64},{64,0},{128,192},{192,128},{1,65},{65,1},{129,193},{193,129... | collective-permute-start | bytes 368648 | tf_op jit(solution)/shard_map/ppermute | solution.py:28
  63.4 2.9 %collective-permute-start.19 = (bf16[96,640]{1,0:T(8,128)(2,1)S(1)}, bf16[96,640]{1,0:T(8,128)(2,1)S(1)}, u32[]{:S(2)}, u32[]{:S(2)}) collective-permute-start(bf16[96,640]{1,0:T(8,128)(2,1)S(1)} %get-tuple-element.88), channel_id=1, source_target_pairs={{0,128},{64,192},{128,0},{192,64},{1,129},{65,193},{129,1},{193,65... | collective-permute-start | bytes 368648 | tf_op jit(solution)/shard_map/ppermute | solution.py:28
  66.9 2.2 %collective-permute-start.14 = (bf16[64,2560]{1,0:T(8,128)(2,1)S(1)}, bf16[64,2560]{1,0:T(8,128)(2,1)S(1)}, u32[]{:S(2)}, u32[]{:S(2)}) collective-permute-start(bf16[64,2560]{1,0:T(8,128)(2,1)S(1)} %get-tuple-element.77), channel_id=1, source_target_pairs={{0,6},{2,4},{4,2},{6,0},{1,7},{3,5},{5,3},{7,1},{8,14},{10,12},{12... | collective-permute-start | bytes 983048 | tf_op jit(solution)/shard_map/ppermute | solution.py:28
  69.1 1.9 %collective-permute-start.15 = (bf16[64,2560]{1,0:T(8,128)(2,1)S(1)}, bf16[64,2560]{1,0:T(8,128)(2,1)S(1)}, u32[]{:S(2)}, u32[]{:S(2)}) collective-permute-start(bf16[64,2560]{1,0:T(8,128)(2,1)S(1)} %get-tuple-element.78), channel_id=1, source_target_pairs={{0,4},{2,6},{4,0},{6,2},{1,5},{3,7},{5,1},{7,3},{8,12},{10,14},{12... | collective-permute-start | bytes 983048 | tf_op jit(solution)/shard_map/ppermute | solution.py:28
  71.0 1.6 %collective-permute-done.19.b = bf16[96,640]{1,0:T(8,128)(2,1)S(1)} collective-permute-done((bf16[96,640]{1,0:T(8,128)(2,1)S(1)}, bf16[96,640]{1,0:T(8,128)(2,1)S(1)}, u32[]{:S(2)}, u32[]{:S(2)}) %collective-permute-start.19) | collective-permute-done | bytes 122912 | tf_op jit(solution)/shard_map/ppermute | solution.py:28
  72.6 2.3 %collective-permute-done.20.c = bf16[96,640]{1,0:T(8,128)(2,1)S(1)} collective-permute-done((bf16[96,640]{1,0:T(8,128)(2,1)S(1)}, bf16[96,640]{1,0:T(8,128)(2,1)S(1)}, u32[]{:S(2)}, u32[]{:S(2)}) %collective-permute-start.20) | collective-permute-done | bytes 122912 | tf_op jit(solution)/shard_map/ppermute | solution.py:28
  75.1 2.4 %collective-permute-start.22 = (bf16[192,256]{1,0:T(8,128)(2,1)S(1)}, bf16[192,256]{1,0:T(8,128)(2,1)S(1)}, u32[]{:S(2)}, u32[]{:S(2)}) collective-permute-start(bf16[192,256]{1,0:T(8,128)(2,1)S(1)} %get-tuple-element.92), channel_id=1, source_target_pairs={{0,32},{16,48},{32,0},{48,16},{1,33},{17,49},{33,1},{49,17},{2,34}... | collective-permute-start | bytes 294920 | tf_op jit(solution)/shard_map/ppermute | solution.py:28
  77.6 3.1 %collective-permute-done.21.a = bf16[192,256]{1,0:T(8,128)(2,1)S(1)} collective-permute-done((bf16[192,256]{1,0:T(8,128)(2,1)S(1)}, bf16[192,256]{1,0:T(8,128)(2,1)S(1)}, u32[]{:S(2)}, u32[]{:S(2)}) %collective-permute-start.21) | collective-permute-done | bytes 98336 | tf_op jit(solution)/shard_map/ppermute | solution.py:28
  80.6 1.0 collective-permute-start.23
  81.6 2.4 %collective-permute-done.22.b = bf16[192,256]{1,0:T(8,128)(2,1)S(1)} collective-permute-done((bf16[192,256]{1,0:T(8,128)(2,1)S(1)}, bf16[192,256]{1,0:T(8,128)(2,1)S(1)}, u32[]{:S(2)}, u32[]{:S(2)}) %collective-permute-start.22) | collective-permute-done | bytes 98336 | tf_op jit(solution)/shard_map/ppermute | solution.py:28
  84.0 3.1 %collective-permute-done.23.c = bf16[192,256]{1,0:T(8,128)(2,1)S(1)} collective-permute-done((bf16[192,256]{1,0:T(8,128)(2,1)S(1)}, bf16[192,256]{1,0:T(8,128)(2,1)S(1)}, u32[]{:S(2)}, u32[]{:S(2)}) %collective-permute-start.23) | collective-permute-done | bytes 98336 | tf_op jit(solution)/shard_map/ppermute | solution.py:28
  87.5 2.2 %collective-permute-start.25 = (bf16[64,160]{1,0:T(8,128)(2,1)S(1)}, bf16[64,160]{1,0:T(8,128)(2,1)S(1)}, u32[]{:S(2)}, u32[]{:S(2)}) collective-permute-start(bf16[64,160]{1,0:T(8,128)(2,1)S(1)} %convert_element_type.62), channel_id=1, source_target_pairs={{0,6},{2,4},{4,2},{6,0},{1,7},{3,5},{5,3},{7,1},{8,14},{10,12},{12... | collective-permute-start | bytes 61448 | tf_op jit(solution)/shard_map/ppermute | solution.py:28
  89.7 1.7 %collective-permute-done.24.a = bf16[64,160]{1,0:T(8,128)(2,1)S(1)} collective-permute-done((bf16[64,160]{1,0:T(8,128)(2,1)S(1)}, bf16[64,160]{1,0:T(8,128)(2,1)S(1)}, u32[]{:S(2)}, u32[]{:S(2)}) %collective-permute-start.24) | collective-permute-done | bytes 20512 | tf_op jit(solution)/shard_map/ppermute | solution.py:28
  91.4 1.5 %collective-permute-start.26 = (bf16[64,160]{1,0:T(8,128)(2,1)S(1)}, bf16[64,160]{1,0:T(8,128)(2,1)S(1)}, u32[]{:S(2)}, u32[]{:S(2)}) collective-permute-start(bf16[64,160]{1,0:T(8,128)(2,1)S(1)} %convert_element_type.62), channel_id=1, source_target_pairs={{0,4},{2,6},{4,0},{6,2},{1,5},{3,7},{5,1},{7,3},{8,12},{10,14},{12... | collective-permute-start | bytes 61448 | tf_op jit(solution)/shard_map/ppermute | solution.py:28
  92.9 3.9 %collective-permute-done.26.c = bf16[64,160]{1,0:T(8,128)(2,1)S(1)} collective-permute-done((bf16[64,160]{1,0:T(8,128)(2,1)S(1)}, bf16[64,160]{1,0:T(8,128)(2,1)S(1)}, u32[]{:S(2)}, u32[]{:S(2)}) %collective-permute-start.26) | collective-permute-done | bytes 20512 | tf_op jit(solution)/shard_map/ppermute | solution.py:28
  96.8 2.5 %collective-permute-start.27 = (bf16[64,160]{1,0:T(8,128)(2,1)S(1)}, bf16[64,160]{1,0:T(8,128)(2,1)S(1)}, u32[]{:S(2)}, u32[]{:S(2)}) collective-permute-start(bf16[64,160]{1,0:T(8,128)(2,1)S(1)} %get-tuple-element.97), channel_id=1, source_target_pairs={{0,8},{8,0},{1,9},{9,1},{2,10},{10,2},{3,11},{11,3},{4,12},{12,4},... | collective-permute-start | bytes 61448 | tf_op jit(solution)/shard_map/ppermute | solution.py:28
  99.3 2.1 %collective-permute-start.30 = (bf16[32,800]{1,0:T(8,128)(2,1)S(1)}, bf16[32,800]{1,0:T(8,128)(2,1)S(1)}, u32[]{:S(2)}, u32[]{:S(2)}) collective-permute-start(bf16[32,800]{1,0:T(8,128)(2,1)S(1)} %get-tuple-element.100.own), channel_id=1, source_target_pairs={{0,128},{64,192},{128,0},{192,64},{1,129},{65,193},{129,1},{193,65... | collective-permute-start | bytes 153608 | tf_op jit(solution)/shard_map/ppermute | solution.py:28
  101.4 2.6 %collective-permute-start.31 = (bf16[32,800]{1,0:T(8,128)(2,1)S(1)}, bf16[32,800]{1,0:T(8,128)(2,1)S(1)}, u32[]{:S(2)}, u32[]{:S(2)}) collective-permute-start(bf16[32,800]{1,0:T(8,128)(2,1)S(1)} %get-tuple-element.100.own), channel_id=1, source_target_pairs={{0,192},{64,128},{128,64},{192,0},{1,193},{65,129},{129,65},{193,1... | collective-permute-start | bytes 153608 | tf_op jit(solution)/shard_map/ppermute | solution.py:28
  104.2 2.0 %collective-permute-start.16 = (bf16[32,2560]{1,0:T(8,128)(2,1)S(1)}, bf16[32,2560]{1,0:T(8,128)(2,1)S(1)}, u32[]{:S(2)}, u32[]{:S(2)}) collective-permute-start(bf16[32,2560]{1,0:T(8,128)(2,1)S(1)} %get-tuple-element.80), channel_id=1, source_target_pairs={{0,40},{8,32},{16,56},{24,48},{32,8},{40,0},{48,24},{56,16},{1,41}... | collective-permute-start | bytes 491528 | tf_op jit(solution)/shard_map/ppermute | solution.py:28
  106.3 0.5 collective-permute-done.31.c
  106.8 0.7 local_out.1
  107.5 0.6 slice_reduce_fusion
  108.1 0.9 shared_out.1
  109.1 4.4 %collective-permute-done.16.got = bf16[32,2560]{1,0:T(8,128)(2,1)S(1)} collective-permute-done((bf16[32,2560]{1,0:T(8,128)(2,1)S(1)}, bf16[32,2560]{1,0:T(8,128)(2,1)S(1)}, u32[]{:S(2)}, u32[]{:S(2)}) %collective-permute-start.16) | collective-permute-done | bytes 163872 | tf_op jit(solution)/shard_map/ppermute | solution.py:28
  113.4 0.7 rows_out.1
  (80 shorter events, 2.6 us)
Async XLA Ops:
  0.6 37.1 %copy-start.6 = (bf16[800,32]{0,1:T(8,128)(2,1)S(1)}, bf16[800,32]{0,1:T(8,128)(2,1)}, u32[]{:S(2)}) copy-start(bf16[800,32]{0,1:T(8,128)(2,1)} %param.22) | copy-start | bytes 153604
  0.7 37.1 %copy-start.2 = (bf16[32,2560]{1,0:T(8,128)(2,1)S(1)}, bf16[32,2560]{1,0:T(8,128)(2,1)}, u32[]{:S(2)}) copy-start(bf16[32,2560]{1,0:T(8,128)(2,1)} %b_down.1) | copy-start | bytes 491524
  0.7 37.0 %copy-start.11 = (f32[800]{0:T(1024)S(1)}, f32[800]{0:T(1024)}, u32[]{:S(2)}) copy-start(f32[800]{0:T(1024)} %param.24) | copy-start | bytes 9604
  0.7 37.0 %copy-start.12 = (f32[800]{0:T(1024)S(1)}, f32[800]{0:T(1024)}, u32[]{:S(2)}) copy-start(f32[800]{0:T(1024)} %param.25) | copy-start | bytes 9604
  0.7 37.0 %copy-start.10 = (f32[2560]{0:T(1024)S(1)}, f32[2560]{0:T(1024)}, u32[]{:S(2)}) copy-start(f32[2560]{0:T(1024)} %param.26) | copy-start | bytes 30724
  0.7 37.1 %copy-start.3 = (bf16[2560,32]{0,1:T(8,128)(2,1)S(1)}, bf16[2560,32]{0,1:T(8,128)(2,1)}, u32[]{:S(2)}) copy-start(bf16[2560,32]{0,1:T(8,128)(2,1)} %param.18) | copy-start | bytes 491524
  0.7 12.8 %collective-permute-start = (bf16[16,2560]{1,0:T(8,128)(2,1)}, bf16[16,2560]{1,0:T(8,128)(2,1)S(1)}, u32[]{:S(2)}, u32[]{:S(2)}) collective-permute-start(bf16[16,2560]{1,0:T(8,128)(2,1)} %param.14), channel_id=1, source_target_pairs={{0,40},{8,32},{16,56},{24,48},{32,8},{40,0},{48,24},{56,16},{1,41}... | collective-permute-start | bytes 245768 | tf_op jit(solution)/shard_map/ppermute | solution.py:28
  8.0 2.2 %copy-start = (bf16[800,2560]{1,0:T(8,128)(2,1)S(1)}, bf16[800,2560]{1,0:T(8,128)(2,1)}, u32[]{:S(2)}) copy-start(bf16[800,2560]{1,0:T(8,128)(2,1)} %d_ref.1) | copy-start | bytes 12288004
  10.2 0.9 copy-start.1
  11.1 0.8 copy-start.5
  11.9 1.6 %copy-start.9 = (bf16[16,2560]{1,0:T(8,128)(2,1)S(1)}, bf16[16,2560]{1,0:T(8,128)(2,1)}, u32[]{:S(2)}) copy-start(bf16[16,2560]{1,0:T(8,128)(2,1)} %param.27) | copy-start | bytes 245764
  11.9 25.8 %copy-start.4 = (bf16[2560,32]{0,1:T(8,128)(2,1)S(1)}, bf16[2560,32]{0,1:T(8,128)(2,1)}, u32[]{:S(2)}) copy-start(bf16[2560,32]{0,1:T(8,128)(2,1)} %param.20) | copy-start | bytes 491524
  11.9 25.8 %copy-start.7 = (bf16[32,800]{1,0:T(8,128)(2,1)S(1)}, bf16[32,800]{1,0:T(8,128)(2,1)}, u32[]{:S(2)}) copy-start(bf16[32,800]{1,0:T(8,128)(2,1)} %b_gate.1) | copy-start | bytes 153604
  11.9 25.9 %copy-start.8 = (bf16[32,800]{1,0:T(8,128)(2,1)S(1)}, bf16[32,800]{1,0:T(8,128)(2,1)}, u32[]{:S(2)}) copy-start(bf16[32,800]{1,0:T(8,128)(2,1)} %b_up.1) | copy-start | bytes 153604
  13.6 9.6 %collective-permute-start.1 = (bf16[18,2560]{1,0:T(8,128)(2,1)S(1)}, bf16[18,2560]{1,0:T(8,128)(2,1)S(1)}, u32[]{:S(2)}, u32[]{:S(2)}) collective-permute-start(bf16[18,2560]{1,0:T(8,128)(2,1)S(1)} %pad_maximum_fusion.1), channel_id=1, source_target_pairs={{0,40},{8,32},{16,56},{24,48},{32,8},{40,0},{48,24},{56,16},{1,41}... | collective-permute-start | bytes 276488 | tf_op jit(solution)/shard_map/ppermute | solution.py:28
  13.8 13.2 %collective-permute-start.5 = (bf16[32,2560]{1,0:T(8,128)(2,1)S(1)}, bf16[32,2560]{1,0:T(8,128)(2,1)S(1)}, u32[]{:S(2)}, u32[]{:S(2)}) collective-permute-start(bf16[32,2560]{1,0:T(8,128)(2,1)S(1)} %get-tuple-element.113), channel_id=1, source_target_pairs={{0,2},{2,0},{4,6},{6,4},{1,3},{3,1},{5,7},{7,5},{8,10},{10,8},{12,... | collective-permute-start | bytes 491528 | tf_op jit(solution)/shard_map/ppermute | solution.py:28
  15.3 12.3 %collective-permute-start.6 = (bf16[32,2560]{1,0:T(8,128)(2,1)S(1)}, bf16[32,2560]{1,0:T(8,128)(2,1)S(1)}, u32[]{:S(2)}, u32[]{:S(2)}) collective-permute-start(bf16[32,2560]{1,0:T(8,128)(2,1)S(1)} %get-tuple-element.113), channel_id=1, source_target_pairs={{0,6},{2,4},{4,2},{6,0},{1,7},{3,5},{5,3},{7,1},{8,14},{10,12},{12... | collective-permute-start | bytes 491528 | tf_op jit(solution)/shard_map/ppermute | solution.py:28
  17.4 10.3 %collective-permute-start.7 = (bf16[32,2560]{1,0:T(8,128)(2,1)S(1)}, bf16[32,2560]{1,0:T(8,128)(2,1)S(1)}, u32[]{:S(2)}, u32[]{:S(2)}) collective-permute-start(bf16[32,2560]{1,0:T(8,128)(2,1)S(1)} %get-tuple-element.113), channel_id=1, source_target_pairs={{0,4},{2,6},{4,0},{6,2},{1,5},{3,7},{5,1},{7,3},{8,12},{10,14},{12... | collective-permute-start | bytes 491528 | tf_op jit(solution)/shard_map/ppermute | solution.py:28
  23.3 7.9 %collective-permute-start.2 = (bf16[34,2560]{1,0:T(8,128)(2,1)S(1)}, bf16[34,2560]{1,0:T(8,128)(2,1)S(1)}, u32[]{:S(2)}, u32[]{:S(2)}) collective-permute-start(bf16[34,2560]{1,0:T(8,128)(2,1)S(1)} %pad_maximum_fusion), channel_id=1, source_target_pairs={{0,2},{2,0},{4,6},{6,4},{1,3},{3,1},{5,7},{7,5},{8,10},{10,8},{12,... | collective-permute-start | bytes 522248 | tf_op jit(solution)/shard_map/ppermute | solution.py:28
  24.9 11.8 %collective-permute-start.3 = (bf16[34,2560]{1,0:T(8,128)(2,1)S(1)}, bf16[34,2560]{1,0:T(8,128)(2,1)S(1)}, u32[]{:S(2)}, u32[]{:S(2)}) collective-permute-start(bf16[34,2560]{1,0:T(8,128)(2,1)S(1)} %pad_maximum_fusion), channel_id=1, source_target_pairs={{0,6},{2,4},{4,2},{6,0},{1,7},{3,5},{5,3},{7,1},{8,14},{10,12},{12... | collective-permute-start | bytes 522248 | tf_op jit(solution)/shard_map/ppermute | solution.py:28
  27.0 9.7 %collective-permute-start.4 = (bf16[34,2560]{1,0:T(8,128)(2,1)S(1)}, bf16[34,2560]{1,0:T(8,128)(2,1)S(1)}, u32[]{:S(2)}, u32[]{:S(2)}) collective-permute-start(bf16[34,2560]{1,0:T(8,128)(2,1)S(1)} %pad_maximum_fusion), channel_id=1, source_target_pairs={{0,4},{2,6},{4,0},{6,2},{1,5},{3,7},{5,1},{7,3},{8,12},{10,14},{12... | collective-permute-start | bytes 522248 | tf_op jit(solution)/shard_map/ppermute | solution.py:28
  27.7 18.1 %collective-permute-start.8 = (bf16[128,2560]{1,0:T(8,128)(2,1)S(1)}, bf16[128,2560]{1,0:T(8,128)(2,1)S(1)}, u32[]{:S(2)}, u32[]{:S(2)}) collective-permute-start(bf16[128,2560]{1,0:T(8,128)(2,1)S(1)} %constant_dynamic-update-slice_fusion.4.mine), channel_id=1, source_target_pairs={{0,1},{1,0},{2,3},{3,2},{4,5},{5,4},{6,7},{7,6},{8,9},{9,8},{10,11... | collective-permute-start | bytes 1966088 | tf_op jit(solution)/shard_map/ppermute | solution.py:28
  36.8 14.8 %collective-permute-start.10 = (bf16[128,2560]{1,0:T(8,128)(2,1)S(1)}, bf16[128,2560]{1,0:T(8,128)(2,1)S(1)}, u32[]{:S(2)}, u32[]{:S(2)}) collective-permute-start(bf16[128,2560]{1,0:T(8,128)(2,1)S(1)} %slice_dynamic-update-slice_fusion.after.cot_mine), channel_id=1, source_target_pairs={{0,1},{1,0},{2,3},{3,2},{4,5},{5,4},{6,7},{7,6},{8,9},{9,8},{10,11... | collective-permute-start | bytes 1966088 | tf_op jit(solution)/shard_map/ppermute | solution.py:28
  36.9 8.9 %collective-permute-start.11 = (f32[1,2560]{1,0:T(1,128)S(1)}, f32[1,2560]{1,0:T(1,128)S(1)}, u32[]{:S(2)}, u32[]{:S(2)}) collective-permute-start(f32[1,2560]{1,0:T(1,128)S(1)} %fusion.2), channel_id=1, source_target_pairs={{0,1},{1,0},{2,3},{3,2},{4,5},{5,4},{6,7},{7,6},{8,9},{9,8},{10,11... | collective-permute-start | bytes 30728 | tf_op jit(solution)/shard_map/ppermute | solution.py:28
  51.3 15.2 %collective-permute-start.9 = (bf16[128,2560]{1,0:T(8,128)(2,1)S(1)}, bf16[128,2560]{1,0:T(8,128)(2,1)S(1)}, u32[]{:S(2)}, u32[]{:S(2)}) collective-permute-start(bf16[128,2560]{1,0:T(8,128)(2,1)S(1)} %get-tuple-element.65.p_away), channel_id=1, source_target_pairs={{0,1},{1,0},{2,3},{3,2},{4,5},{5,4},{6,7},{7,6},{8,9},{9,8},{10,11... | collective-permute-start | bytes 1966088 | tf_op jit(solution)/shard_map/ppermute | solution.py:28
  58.9 7.6 %collective-permute-start.12 = (bf16[128,2560]{1,0:T(8,128)(2,1)S(1)}, bf16[128,2560]{1,0:T(8,128)(2,1)S(1)}, u32[]{:S(2)}, u32[]{:S(2)}) collective-permute-start(bf16[128,2560]{1,0:T(8,128)(2,1)S(1)} %get-tuple-element.74), channel_id=1, source_target_pairs={{0,1},{1,0},{2,3},{3,2},{4,5},{5,4},{6,7},{7,6},{8,9},{9,8},{10,11... | collective-permute-start | bytes 1966088 | tf_op jit(solution)/shard_map/ppermute | solution.py:28
  59.4 2.2 %collective-permute-start.17 = (bf16[4,64,640]{2,1,0:T(8,128)(2,1)S(1)}, bf16[4,64,640]{2,1,0:T(8,128)(2,1)S(1)}, u32[]{:S(2)}, u32[]{:S(2)}) collective-permute-start(bf16[4,64,640]{2,1,0:T(8,128)(2,1)S(1)} %get-tuple-element.84), channel_id=1, source_target_pairs={{0,1},{1,0},{2,3},{3,2},{4,5},{5,4},{6,7},{7,6},{8,9},{9,8},{10,11... | collective-permute-start | bytes 983048 | tf_op jit(solution)/shard_map/ppermute | solution.py:28
  61.7 7.4 %collective-permute-start.18 = (bf16[96,640]{1,0:T(8,128)(2,1)S(1)}, bf16[96,640]{1,0:T(8,128)(2,1)S(1)}, u32[]{:S(2)}, u32[]{:S(2)}) collective-permute-start(bf16[96,640]{1,0:T(8,128)(2,1)S(1)} %get-tuple-element.87), channel_id=1, source_target_pairs={{0,64},{64,0},{128,192},{192,128},{1,65},{65,1},{129,193},{193,129... | collective-permute-start | bytes 368648 | tf_op jit(solution)/shard_map/ppermute | solution.py:28
  63.4 9.2 %collective-permute-start.19 = (bf16[96,640]{1,0:T(8,128)(2,1)S(1)}, bf16[96,640]{1,0:T(8,128)(2,1)S(1)}, u32[]{:S(2)}, u32[]{:S(2)}) collective-permute-start(bf16[96,640]{1,0:T(8,128)(2,1)S(1)} %get-tuple-element.88), channel_id=1, source_target_pairs={{0,128},{64,192},{128,0},{192,64},{1,129},{65,193},{129,1},{193,65... | collective-permute-start | bytes 368648 | tf_op jit(solution)/shard_map/ppermute | solution.py:28
  66.3 8.6 %collective-permute-start.20 = (bf16[96,640]{1,0:T(8,128)(2,1)S(1)}, bf16[96,640]{1,0:T(8,128)(2,1)S(1)}, u32[]{:S(2)}, u32[]{:S(2)}) collective-permute-start(bf16[96,640]{1,0:T(8,128)(2,1)S(1)} %get-tuple-element.89), channel_id=1, source_target_pairs={{0,192},{64,128},{128,64},{192,0},{1,193},{65,129},{129,65},{193,1... | collective-permute-start | bytes 368648 | tf_op jit(solution)/shard_map/ppermute | solution.py:28
  66.8 32.5 %collective-permute-start.13 = (bf16[64,2560]{1,0:T(8,128)(2,1)S(1)}, bf16[64,2560]{1,0:T(8,128)(2,1)S(1)}, u32[]{:S(2)}, u32[]{:S(2)}) collective-permute-start(bf16[64,2560]{1,0:T(8,128)(2,1)S(1)} %get-tuple-element.76), channel_id=1, source_target_pairs={{0,2},{2,0},{4,6},{6,4},{1,3},{3,1},{5,7},{7,5},{8,10},{10,8},{12,... | collective-permute-start | bytes 983048 | tf_op jit(solution)/shard_map/ppermute | solution.py:28
  66.9 34.5 %collective-permute-start.14 = (bf16[64,2560]{1,0:T(8,128)(2,1)S(1)}, bf16[64,2560]{1,0:T(8,128)(2,1)S(1)}, u32[]{:S(2)}, u32[]{:S(2)}) collective-permute-start(bf16[64,2560]{1,0:T(8,128)(2,1)S(1)} %get-tuple-element.77), channel_id=1, source_target_pairs={{0,6},{2,4},{4,2},{6,0},{1,7},{3,5},{5,3},{7,1},{8,14},{10,12},{12... | collective-permute-start | bytes 983048 | tf_op jit(solution)/shard_map/ppermute | solution.py:28
  69.1 34.9 %collective-permute-start.15 = (bf16[64,2560]{1,0:T(8,128)(2,1)S(1)}, bf16[64,2560]{1,0:T(8,128)(2,1)S(1)}, u32[]{:S(2)}, u32[]{:S(2)}) collective-permute-start(bf16[64,2560]{1,0:T(8,128)(2,1)S(1)} %get-tuple-element.78), channel_id=1, source_target_pairs={{0,4},{2,6},{4,0},{6,2},{1,5},{3,7},{5,1},{7,3},{8,12},{10,14},{12... | collective-permute-start | bytes 983048 | tf_op jit(solution)/shard_map/ppermute | solution.py:28
  75.0 5.6 %collective-permute-start.21 = (bf16[192,256]{1,0:T(8,128)(2,1)S(1)}, bf16[192,256]{1,0:T(8,128)(2,1)S(1)}, u32[]{:S(2)}, u32[]{:S(2)}) collective-permute-start(bf16[192,256]{1,0:T(8,128)(2,1)S(1)} %get-tuple-element.91), channel_id=1, source_target_pairs={{0,16},{16,0},{32,48},{48,32},{1,17},{17,1},{33,49},{49,33},{2,18}... | collective-permute-start | bytes 294920 | tf_op jit(solution)/shard_map/ppermute | solution.py:28
  75.1 8.8 %collective-permute-start.22 = (bf16[192,256]{1,0:T(8,128)(2,1)S(1)}, bf16[192,256]{1,0:T(8,128)(2,1)S(1)}, u32[]{:S(2)}, u32[]{:S(2)}) collective-permute-start(bf16[192,256]{1,0:T(8,128)(2,1)S(1)} %get-tuple-element.92), channel_id=1, source_target_pairs={{0,32},{16,48},{32,0},{48,16},{1,33},{17,49},{33,1},{49,17},{2,34}... | collective-permute-start | bytes 294920 | tf_op jit(solution)/shard_map/ppermute | solution.py:28
  80.6 6.4 %collective-permute-start.23 = (bf16[192,256]{1,0:T(8,128)(2,1)S(1)}, bf16[192,256]{1,0:T(8,128)(2,1)S(1)}, u32[]{:S(2)}, u32[]{:S(2)}) collective-permute-start(bf16[192,256]{1,0:T(8,128)(2,1)S(1)} %get-tuple-element.93), channel_id=1, source_target_pairs={{0,48},{16,32},{32,16},{48,0},{1,49},{17,33},{33,17},{49,1},{2,50}... | collective-permute-start | bytes 294920 | tf_op jit(solution)/shard_map/ppermute | solution.py:28
  87.1 4.3 %collective-permute-start.24 = (bf16[64,160]{1,0:T(8,128)(2,1)S(1)}, bf16[64,160]{1,0:T(8,128)(2,1)S(1)}, u32[]{:S(2)}, u32[]{:S(2)}) collective-permute-start(bf16[64,160]{1,0:T(8,128)(2,1)S(1)} %convert_element_type.62), channel_id=1, source_target_pairs={{0,2},{2,0},{4,6},{6,4},{1,3},{3,1},{5,7},{7,5},{8,10},{10,8},{12,... | collective-permute-start | bytes 61448 | tf_op jit(solution)/shard_map/ppermute | solution.py:28
  87.5 5.4 %collective-permute-start.25 = (bf16[64,160]{1,0:T(8,128)(2,1)S(1)}, bf16[64,160]{1,0:T(8,128)(2,1)S(1)}, u32[]{:S(2)}, u32[]{:S(2)}) collective-permute-start(bf16[64,160]{1,0:T(8,128)(2,1)S(1)} %convert_element_type.62), channel_id=1, source_target_pairs={{0,6},{2,4},{4,2},{6,0},{1,7},{3,5},{5,3},{7,1},{8,14},{10,12},{12... | collective-permute-start | bytes 61448 | tf_op jit(solution)/shard_map/ppermute | solution.py:28
  91.4 5.4 %collective-permute-start.26 = (bf16[64,160]{1,0:T(8,128)(2,1)S(1)}, bf16[64,160]{1,0:T(8,128)(2,1)S(1)}, u32[]{:S(2)}, u32[]{:S(2)}) collective-permute-start(bf16[64,160]{1,0:T(8,128)(2,1)S(1)} %convert_element_type.62), channel_id=1, source_target_pairs={{0,4},{2,6},{4,0},{6,2},{1,5},{3,7},{5,1},{7,3},{8,12},{10,14},{12... | collective-permute-start | bytes 61448 | tf_op jit(solution)/shard_map/ppermute | solution.py:28
  96.8 9.3 %collective-permute-start.27 = (bf16[64,160]{1,0:T(8,128)(2,1)S(1)}, bf16[64,160]{1,0:T(8,128)(2,1)S(1)}, u32[]{:S(2)}, u32[]{:S(2)}) collective-permute-start(bf16[64,160]{1,0:T(8,128)(2,1)S(1)} %get-tuple-element.97), channel_id=1, source_target_pairs={{0,8},{8,0},{1,9},{9,1},{2,10},{10,2},{3,11},{11,3},{4,12},{12,4},... | collective-permute-start | bytes 61448 | tf_op jit(solution)/shard_map/ppermute | solution.py:28
  99.3 6.9 %collective-permute-start.29 = (bf16[32,800]{1,0:T(8,128)(2,1)S(1)}, bf16[32,800]{1,0:T(8,128)(2,1)S(1)}, u32[]{:S(2)}, u32[]{:S(2)}) collective-permute-start(bf16[32,800]{1,0:T(8,128)(2,1)S(1)} %get-tuple-element.100.own), channel_id=1, source_target_pairs={{0,64},{64,0},{128,192},{192,128},{1,65},{65,1},{129,193},{193,129... | collective-permute-start | bytes 153608 | tf_op jit(solution)/shard_map/ppermute | solution.py:28
  99.3 6.9 %collective-permute-start.30 = (bf16[32,800]{1,0:T(8,128)(2,1)S(1)}, bf16[32,800]{1,0:T(8,128)(2,1)S(1)}, u32[]{:S(2)}, u32[]{:S(2)}) collective-permute-start(bf16[32,800]{1,0:T(8,128)(2,1)S(1)} %get-tuple-element.100.own), channel_id=1, source_target_pairs={{0,128},{64,192},{128,0},{192,64},{1,129},{65,193},{129,1},{193,65... | collective-permute-start | bytes 153608 | tf_op jit(solution)/shard_map/ppermute | solution.py:28
  101.4 5.4 %collective-permute-start.31 = (bf16[32,800]{1,0:T(8,128)(2,1)S(1)}, bf16[32,800]{1,0:T(8,128)(2,1)S(1)}, u32[]{:S(2)}, u32[]{:S(2)}) collective-permute-start(bf16[32,800]{1,0:T(8,128)(2,1)S(1)} %get-tuple-element.100.own), channel_id=1, source_target_pairs={{0,192},{64,128},{128,64},{192,0},{1,193},{65,129},{129,65},{193,1... | collective-permute-start | bytes 153608 | tf_op jit(solution)/shard_map/ppermute | solution.py:28
  104.2 9.3 %collective-permute-start.16 = (bf16[32,2560]{1,0:T(8,128)(2,1)S(1)}, bf16[32,2560]{1,0:T(8,128)(2,1)S(1)}, u32[]{:S(2)}, u32[]{:S(2)}) collective-permute-start(bf16[32,2560]{1,0:T(8,128)(2,1)S(1)} %get-tuple-element.80), channel_id=1, source_target_pairs={{0,40},{8,32},{16,56},{24,48},{32,8},{40,0},{48,24},{56,16},{1,41}... | collective-permute-start | bytes 491528 | tf_op jit(solution)/shard_map/ppermute | solution.py:28
  106.1 2.0 %collective-permute-start.28 = (f32[64,160]{1,0:T(8,128)S(1)}, f32[64,160]{1,0:T(8,128)S(1)}, u32[]{:S(2)}, u32[]{:S(2)}) collective-permute-start(f32[64,160]{1,0:T(8,128)S(1)} %convert_add_fusion.own), channel_id=1, source_target_pairs={{0,1},{1,0},{2,3},{3,2},{4,5},{5,4},{6,7},{7,6},{8,9},{9,8},{10,11... | collective-permute-start | bytes 122888 | tf_op jit(solution)/shard_map/ppermute | solution.py:28
where the time goes:
time: 114 us
  starting transfers between devices  41.8 us (37%)
  waiting for transfers between devices  39.1 us (34%)
  Pallas kernels  25.4 us (22%)
  local copies, waits for them, and re-layouts  6.49 us (6%)
    ppermute x32, starting transfers between devices, swap(): return lax.ppermute(value, axis, [(i, i ^ distance) for i in range(size)])  41.8 us
    ppermute x32, waiting for transfers between devices, swap(): return lax.ppermute(value, axis, [(i, i ^ distance) for i in range(size)])  39.1 us
    pallas_call x1, Pallas kernels, merge(): call(merge_kernel, 'merge', [shape(*gate.shape)] * 3 + [shape(1, units, d...  7.97 us
    unnamed x32, local copies, waits for them, and re-layouts  5.81 us
    pallas_call x1, Pallas kernels, forward(): call(forward_kernel, 'forward', [shape(half, features)] * 2 + [shape(2 *...  5.44 us
    pallas_call x1, Pallas kernels, backward(): call(backward_kernel, 'backward', [shape(2 * half, units)] * 2 + [shape(4...  4.04 us
    pallas_call x1, Pallas kernels, input_gradient_of(): call(input_gradient_kernel, 'input_gradient', [shape(rows, gate.shape[1])...  3.3 us
  transfers between devices with their start and end apart: 32, of which 13 were waited for; matrix products, arithmetic and copies ran while one was open for 2% of the time, Pallas kernels for 22%

commit v1 on v0

--- a/solution.py
+++ b/solution.py
@@ -71,23 +71,6 @@
     return [pl.ds(i, WIDE) for i in range(0, features, WIDE)]
 
 
-def down_squares_kernel(w_ref, a_ref, b_ref, squares_ref):
-    for part in parts(w_ref.shape[1]):
-        merged = w_ref[:, part].astype(f32) + adapter_scale * dot_first(a_ref[...], b_ref[:, part])
-        squares_ref[:, part] = jnp.sum(merged * merged, axis=0, keepdims=True)
-
-
-def down_squares(weight, left_t, right):
-    return call(
-        down_squares_kernel,
-        "down_squares",
-        shape(1, weight.shape[1], dtype=f32),
-        6,
-        in_specs=[VMEM] * 3,
-        out_specs=VMEM,
-    )(weight, left_t, right)
-
-
 class Copies:
     def __init__(self, pairs, sems, ahead):
         self.copies = [pltpu.make_async_copy(a, b, sems.at[i]) for i, (a, b) in enumerate(pairs)]
@@ -106,27 +89,58 @@
         self.fill()
 
 
+def down_squares_kernel(w_ref, a_ref, b_ref, squares_ref, w, a, b, sems):
+    spans = parts(w_ref.shape[1])
+    pairs = [(a_ref, a), (b_ref, b)] + [(w_ref.at[:, part], w.at[:, part]) for part in spans]
+    copies = Copies(pairs, sems, len(pairs))
+    copies.wait()
+    copies.wait()
+    for part in spans:
+        copies.wait()
+        merged = w[:, part].astype(f32) + adapter_scale * dot_first(a[...], b[:, part])
+        squares_ref[:, part] = jnp.sum(merged * merged, axis=0, keepdims=True)
+
+
+def down_squares(weight, left_t, right):
+    return call(
+        down_squares_kernel,
+        "down_squares",
+        shape(1, weight.shape[1], dtype=f32),
+        56,
+        in_specs=[ANY] * 3,
+        out_specs=VMEM,
+        scratch_shapes=[
+            pltpu.VMEM(weight.shape, bf16),
+            pltpu.VMEM(left_t.shape, bf16),
+            pltpu.VMEM(right.shape, bf16),
+            pltpu.SemaphoreType.DMA((2 + weight.shape[1] // WIDE,)),
+        ],
+    )(weight, left_t, right)
+
+
 def merge_kernel(
     after, g_ref, u_ref, d_ref, ga, ua, gb, ub, ad, bd, g_m, u_m, g_out, u_out, d_out, g_scale, u_scale,
     g_held, u_held, d_held, sems,
 ):
     spans = parts(g_ref.shape[1])
     pairs = []
-    for ref, held in ((g_ref, g_held), (u_ref, u_held), (d_ref, d_held)):
-        pairs += [(ref.at[:, part], held.at[:, part]) for part in spans]
-    copies = Copies(pairs, sems, 6)
+    for part in (pl.ds(0, 2 * WIDE), pl.ds(2 * WIDE, 2 * WIDE)):
+        pairs.append((g_ref.at[:, part], g_held.at[:, part]))
+    pairs += [(u_ref, u_held), (d_ref, d_held)]
+    copies = Copies(pairs, sems, len(pairs))
     for w, a, b, m, out, scale in ((g_held, ga, gb, g_m, g_out, g_scale), (u_held, ua, ub, u_m, u_out, u_scale)):
         squares = 0.0
-        for part in spans:
-            copies.wait()
+        for n, part in enumerate(spans):
+            if n == 0 or (n == 2 and w is g_held):
+                copies.wait()
             merged = w[:, part].astype(f32) + adapter_scale * dot_first(b[...], a[:, part])
             out[:, part] = merged.astype(bf16)
             square = merged * merged
             squares += sum(square[:, k : k + 128] for k in range(0, WIDE, 128))
         total = jnp.sum(jnp.transpose(squares), axis=0, keepdims=True)
         scale[...] = m[...] / jnp.sqrt(total + epsilon)
+    copies.wait()
     for part in spans:
-        copies.wait()
         merged = d_held[:, part].astype(f32) + adapter_scale * dot_first(ad[...], bd[:, part])
         d_out[:, part] = merged.astype(bf16)
 
@@ -140,7 +154,7 @@
         40,
         in_specs=[ANY] * 4 + [VMEM] * len(others),
         out_specs=[VMEM] * 5,
-        scratch_shapes=[pltpu.VMEM(gate.shape, bf16)] * 3 + [pltpu.SemaphoreType.DMA((3 * (features // WIDE),))],
+        scratch_shapes=[pltpu.VMEM(gate.shape, bf16)] * 3 + [pltpu.SemaphoreType.DMA((4,))],
     )(after, gate, up, down, *others)
 
 
@@ -285,7 +299,8 @@
     )(delta_gate, delta_up, gate, up)
 
 
-def core_sum_kernel(after, own, got, local, out0, out1, out2, out3):
+def core_sum_kernel(away, own, got, local, away_out, out0, out1, out2, out3):
+    away_out[...] = away[...]
     for k, out in enumerate((out0, out1, out2, out3)):
         total = own[k].astype(f32) + got[k].astype(f32)
         folded = local[k, pl.ds(RANK, 16), :].astype(f32)
@@ -293,15 +308,15 @@
         out[pl.ds(SHARED, RANK), :] = local[k, pl.ds(0, RANK), :]
 
 
-def core_sum(after, own, got, local):
+def core_sum(away, own, got, local):
     return call(
         core_sum_kernel,
         "core_sum",
-        [shape(SHARED + RANK, own.shape[2])] * 4,
+        [shape(*away.shape)] + [shape(SHARED + RANK, own.shape[2])] * 4,
         4,
-        in_specs=[ANY] + [VMEM] * 3,
-        out_specs=[VMEM] * 4,
-    )(after, own, got, local)
+        in_specs=[VMEM] * 4,
+        out_specs=[VMEM] * 5,
+    )(away, own, got, local)
 
 
 def after_y_kernel(zl, after, own, a, b, c, out0, out1, out2, out3, shared):
@@ -314,114 +329,71 @@
     folded = total[SHARED - 8 : SHARED]
     rest = jnp.concatenate([folded[:, i * quarter : (i + 1) * quarter] for i in range(4)], axis=0)
     local = jnp.concatenate([total[SHARED:], rest], axis=1).astype(bf16)
+    rest = local[:, 3 * wide :].astype(f32)
+    rest = jnp.concatenate([rest, jnp.zeros((SHARED - RANK, rest.shape[1]), f32)], axis=0)
+    shared[4, :, pl.ds(0, 128)] = jnp.zeros((SHARED, 128), f32)
+    shared[4, :, pl.ds(128, 128)] = jnp.zeros((SHARED, 128), f32)
+    shared[4, :, pl.ds(0, rest.shape[1])] = rest
+    rest = pltpu.roll(shared[4], quarter, 1)
+    lane = lax.broadcasted_iota(jnp.int32, rest.shape, 1)
     for k, out in enumerate((out0, out1, out2, out3)):
-        out[pl.ds(0, SHARED), :] = shared[here ^ k].astype(bf16)
+        out[pl.ds(0, SHARED), :] = jnp.where(lane < quarter, shared[here ^ k], rest).astype(bf16)
         for i in range(3):
             out[pl.ds(SHARED + i * RANK, RANK), :] = local[:, i * wide : (i + 1) * wide]
-        out[pl.ds(SHARED + 3 * RANK, RANK), pl.ds(0, local.shape[1] - 3 * wide)] = local[:, 3 * wide :]
 
 
 def after_y(zl, after, own, others):
     return call(
         after_y_kernel,
         "after_y",
-        [shape(SHARED + 4 * RANK, 256)] * 4,
+        [shape(SHARED + 3 * RANK, 256)] * 4,
         4,
+        flops=3000000000,
         in_specs=[SMEM, ANY] + [VMEM] * 4,
         out_specs=[VMEM] * 4,
-        scratch_shapes=[pltpu.VMEM((4, SHARED, 256), f32)],
+        scratch_shapes=[pltpu.VMEM((5, SHARED, 256), f32)],
     )(zl, after, own, *others)
 
 
-def after_z_kernel(own, a, b, c, shared, local):
+def after_z_kernel(after, own, a, b, c, shared, local):
     total = own[...].astype(f32) + a[...].astype(f32) + b[...].astype(f32) + c[...].astype(f32)
     shared[...] = total[:SHARED, : shared.shape[1]]
     wide = own.shape[1]
-    for i in range(4):
-        width = min(wide, local.shape[1] - i * wide)
+    for i in range(3):
         first = SHARED + i * RANK
-        local[:, pl.ds(i * wide, width)] = total[first : first + RANK, :width].astype(bf16)
-
-
-def after_z(own, others, quarter, units):
+        local[:, pl.ds(i * wide, wide)] = total[first : first + RANK].astype(bf16)
+    quarter = shared.shape[1]
+    width = local.shape[1] - 3 * wide
+    local[:, pl.ds(3 * wide, width)] = total[:RANK, quarter : quarter + width].astype(bf16)
+
+
+def after_z(after, own, others, quarter, units):
     return call(
         after_z_kernel,
         "after_z",
         [shape(SHARED, quarter, dtype=f32), shape(RANK, units)],
         4,
-        in_specs=[VMEM] * 4,
+        flops=3000000000,
+        in_specs=[ANY] + [VMEM] * 4,
         out_specs=[VMEM] * 2,
-    )(own, *others)
-
-
-def x_sum_kernel(own, a, b, c, local, out, sent, local_out):
+    )(after, own, *others)
+
+
+def x_sum_kernel(after, own, a, b, c, out, sent):
     total = own[...] + a[...].astype(f32) + b[...].astype(f32) + c[...].astype(f32)
     out[...] = total
     sent[...] = total.astype(bf16)
-    local_out[...] = local[...]
-
-
-def x_sum(own, others, local):
+
+
+def x_sum(after, own, others):
     return call(
         x_sum_kernel,
         "x_sum",
-        [shape(*own.shape, dtype=f32), shape(*own.shape), shape(*local.shape)],
+        [shape(*own.shape, dtype=f32), shape(*own.shape)],
         4,
-        in_specs=[VMEM] * 5,
-        out_specs=[VMEM] * 3,
-    )(own, *others, local)
-
-
-def local_out_kernel(y, own, a, b, c, gate, up, down, stats, held):
-    for k, piece in enumerate((own, a, b, c)):
-        held[k] = piece[...]
-    here = y[0]
-    for j, out in enumerate((gate, up, down)):
-        out[...] = held[here ^ j].astype(f32)
-    stats[...] = held[here ^ 3][:8].astype(f32)
-
-
-def local_out(y, own, others):
-    units = own.shape[1]
-    return call(
-        local_out_kernel,
-        "local_out",
-        [shape(RANK, units, dtype=f32)] * 3 + [shape(8, units, dtype=f32)],
-        4,
-        in_specs=[SMEM] + [VMEM] * 4,
-        out_specs=[VMEM] * 4,
-        scratch_shapes=[pltpu.VMEM((4, RANK, units), bf16)],
-    )(y, own, *others)
-
-
-def shared_out_kernel(place, core, own, got, gate, up, down, moment):
-    wide = gate.shape[0]
-    first = core[0] == 0
-    halves = jnp.where(first, own[...], got[...]), jnp.where(first, got[...], own[...])
-    spots = (16, own.shape[1])
-    row = lax.broadcasted_iota(jnp.int32, spots, 0)
-    chosen = (lax.broadcasted_iota(jnp.int32, spots, 1) == place[0] * wide + row).astype(f32)
-    highest = lax.Precision.HIGHEST
-    last = (((1,), (1,)), ((), ()))
-    one, two = [lax.dot_general(chosen, h, last, precision=highest, preferred_element_type=f32) for h in halves]
-    gate[...] = one[:wide, :RANK]
-    up[...] = two[:wide, :RANK]
-    down[:, pl.ds(0, 16)] = one[:wide, RANK : RANK + 16]
-    down[:, pl.ds(16, 16)] = two[:wide, RANK : RANK + 16]
-    line = lax.dot_general(halves[1][48:56], chosen, last, precision=highest, preferred_element_type=f32)
-    moment[...] = line[:1, :wide]
-
-
-def shared_out(place, core, own, got):
-    wide = own.shape[1] // 16
-    return call(
-        shared_out_kernel,
-        "shared_out",
-        [shape(wide, RANK, dtype=f32)] * 3 + [shape(1, wide, dtype=f32)],
-        4,
-        in_specs=[SMEM] * 2 + [VMEM] * 2,
-        out_specs=[VMEM] * 4,
-    )(place, core, own, got)
+        in_specs=[ANY] + [VMEM] * 4,
+        out_specs=[VMEM] * 2,
+    )(after, own, *others)
 
 
 def half_sum_kernel(p_mine, p_got, i_mine, i_got, pair, one, two, three):
@@ -468,24 +440,73 @@
     )(pair, *got)
 
 
-def rows_out_kernel(own, got, d_sq, m_down, outputs, input_gradient):
+def finish_kernel(
+    y, place, core, row_own, row_got, d_sq, m_down, shared, shared_got, own, a, b, c,
+    outputs, input_gradient, gate_in, up_in, gate, up, down, down_in, gate_m, up_m, down_m, held,
+):
     rows = outputs.shape[0]
-    total = own[...] + got[...].astype(f32)
+    total = row_own[...] + row_got[...].astype(f32)
     scale_down = m_down[...] / jnp.sqrt(d_sq[...] + epsilon)
     outputs[...] = (total[:rows] * scale_down).astype(bf16)
     input_gradient[...] = total[rows:].astype(bf16)
-
-
-def rows_out(own, got, d_sq, m_down):
-    rows, features = own.shape
-    return call(
-        rows_out_kernel,
-        "rows_out",
-        [shape(rows // 2, features)] * 2,
+    for k, piece in enumerate((own, a, b, c)):
+        held[k] = piece[...]
+    here = y[0]
+    for j, out in enumerate((gate, up, down)):
+        out[...] = held[here ^ j].astype(f32)
+    stats = held[here ^ 3][:16].astype(f32)
+    gate_m[...] = stats[0]
+    up_m[...] = stats[1]
+    wide = gate_in.shape[0]
+    first = core[0] == 0
+    halves = jnp.where(first, shared[...], shared_got[...]), jnp.where(first, shared_got[...], shared[...])
+    spots = (16, shared.shape[1])
+    row = lax.broadcasted_iota(jnp.int32, spots, 0)
+    chosen = (lax.broadcasted_iota(jnp.int32, spots, 1) == place[0] * wide + row).astype(f32)
+    highest = lax.Precision.HIGHEST
+    last = (((1,), (1,)), ((), ()))
+    one, two = [lax.dot_general(chosen, h, last, precision=highest, preferred_element_type=f32) for h in halves]
+    gate_in[...] = one[:wide, :RANK]
+    up_in[...] = two[:wide, :RANK]
+    down_in[:, pl.ds(0, 16)] = one[:wide, RANK : RANK + 16]
+    down_in[:, pl.ds(16, 16)] = two[:wide, RANK : RANK + 16]
+    line = lax.dot_general(halves[1][48:56], chosen, last, precision=highest, preferred_element_type=f32)
+    down_m[...] = line[:1, :wide]
+
+
+def finish(y, place, core, row_own, row_got, d_sq, m_down, shared, shared_got, own, others):
+    rows, features = row_own.shape
+    wide = shared.shape[1] // 16
+    units = own.shape[1]
+    small = shape(wide, RANK, dtype=f32)
+    local = shape(RANK, units, dtype=f32)
+    line = shape(units, dtype=f32)
+    return call(
+        finish_kernel,
+        "finish",
+        [shape(rows // 2, features)] * 2 + [small] * 2 + [local] * 3 + [small, line, line, shape(1, wide, dtype=f32)],
+        6,
+        in_specs=[SMEM] * 3 + [VMEM] * 10,
+        out_specs=[VMEM] * 11,
+        scratch_shapes=[pltpu.VMEM((4, RANK, units), bf16)],
+    )(y, place, core, row_own, row_got, d_sq, m_down, shared, shared_got, own, *others)
+
+
+def join_cot_kernel(after, pair, a, b, c, out):
+    rows = pair.shape[0]
+    for i, piece in enumerate((pair, a, b, c)):
+        out[pl.ds(i * rows, rows), :] = piece[:rows]
+
+
+def join_cot(after, pair, got):
+    return call(
+        join_cot_kernel,
+        "join_cot",
+        shape(4 * pair.shape[0], pair.shape[1]),
         4,
-        in_specs=[VMEM] * 4,
-        out_specs=[VMEM] * 2,
-    )(own, got, d_sq, m_down)
+        in_specs=[ANY] + [VMEM] * 4,
+        out_specs=VMEM,
+    )(after, pair, *got)
 
 
 def held_until_kernel(after, value, out):
@@ -525,7 +546,9 @@
     ga_t, ua_t, ad_t = gate_adapter_in.T, upper_adapter_in.T, down_adapter_in.T
 
     other = swap_z(inputs)
-    squares = held_until(other, down_squares(down_weight, ad_t, b_down))
+    squares = down_squares(down_weight, ad_t, b_down)
+    squares = held_until(other, squares)
+    squares = squares + swap_core(squares)
     got = swap_z(jnp.concatenate([cotangent, split(squares)], axis=0))
     pair = jnp.concatenate([inputs, other], axis=0)
     got_x = swap_x(pair)
@@ -535,14 +558,12 @@
     got = swap_x(jnp.concatenate([pair, split(squares)], axis=0))
 
     gate, up, down, g_scale, u_scale = merge(
-        got_x[0], gate_t, up_t, down_weight, ga_t, ua_t, b_gate, b_up, ad_t, b_down, m_gate, m_up
+        mine, gate_t, up_t, down_weight, ga_t, ua_t, b_gate, b_up, ad_t, b_down, m_gate, m_up
     )
     away = swap_core(mine)
-    cot_mine = jnp.concatenate([pair] + [g[: 2 * rows] for g in got], axis=0)
+    cot_mine = join_cot(g_scale, pair, got)
     cot_away = swap_core(cot_mine)
     squares = squares + sum(joined(g[2 * rows :]) for g in got)
-    squares = squares + swap_core(squares)
-
     p_mine, p_away, hidden, gate_value, up_value, rank_in_t, rank_down_t = forward(
         cot_mine, mine, away, gate, up, down, ga_t, ua_t, ad_t, g_scale, u_scale
     )
@@ -553,20 +574,21 @@
         rank_in_t, rank_down_t, b_down, b_gate, b_up, g_scale, u_scale, m_gate, m_up, squares, m_down,
     )
     i_mine, i_away = input_gradient_of(delta_gate, delta_up, gate, up)
-    packed = core_sum(i_mine, shared_own, swap_core(shared_away), local)
+    i_away, *packed = core_sum(i_away, shared_own, swap_core(shared_away), local)
     pair, *sent = half_sum(p_mine, p_got, i_mine, swap_core(i_away))
     own, *sent_z = after_y(zl, pair, packed[0], [swap(packed[k], "y", k, 4) for k in (1, 2, 3)])
 
+    row_own, sent = pair_sum(pair, [swap(v, "x", k, 4) for k, v in zip(X_ORDER, sent)])
+    row_got = swap_z(sent)
+
     quarter = features // 16
-    shared, local = after_z(own, [swap(v, "zl", k + 1, 4) for k, v in enumerate(sent_z)], quarter, units)
-    shared, sent_zh, local = x_sum(shared, swap_x(shared.astype(bf16)), local)
+    shared, local = after_z(packed[0], own, [swap(v, "zl", k + 1, 4) for k, v in enumerate(sent_z)], quarter, units)
+    others = [swap(local, "y", k, 4) for k in (1, 2, 3)]
+    shared, sent_zh = x_sum(row_got, shared, swap_x(shared.astype(bf16)))
     shared = shared + swap(sent_zh, "zh", 1, 2).astype(f32)
-    gate_in, up_in, down_in, moment = shared_out(place[None], core, shared, swap_core(shared))
-    gate_out, up_out, down_out, stats = local_out(y, local, [swap(local, "y", k, 4) for k in (1, 2, 3)])
-
-    own, sent = pair_sum(pair, [swap(v, "x", k, 4) for k, v in zip(X_ORDER, sent)])
-    outputs, input_gradient = rows_out(own, swap_z(sent), squares, m_down)
-
+    outputs, input_gradient, gate_in, up_in, gate_out, up_out, down_out, down_in, gate_m, up_m, down_m = finish(
+        y, place[None], core, row_own, row_got, squares, m_down, shared, swap_core(shared), local, others
+    )
     return (
         outputs,
         input_gradient,
@@ -576,9 +598,9 @@
         up_out,
         down_out.T,
         down_in.T,
-        stats[0],
-        stats[1],
-        moment[0],
+        gate_m,
+        up_m,
+        down_m[0],
     )
 
 

time: 114 us -> 98.9 us (0.87)
  waiting for transfers between devices: 39.1 us -> 26.1 us
  local copies, waits for them, and re-layouts: 6.49 us -> 0.84 us
  starting transfers between devices: 41.8 us -> 44.8 us
    ppermute x32, waiting for transfers between devices: 39.1 us -> 26.1 us  [swap(): return lax.ppermute(value, axis, [(i, i ^ distance) for i in range(size)])]
    unnamed x32 -> x27, local copies, waits for them, and re-layouts: 5.81 us -> 0.79 us
    ppermute x32, starting transfers between devices: 41.8 us -> 44.8 us  [swap(): return lax.ppermute(value, axis, [(i, i ^ distance) for i in range(size)])]
    pallas_call x1, Pallas kernels: 1.59 us -> 4.2 us  [down_squares(): call(down_squares_kernel, 'down_squares', shape(1, weight.shape[1], dtype...]
    pallas_call x1, Pallas kernels: 7.97 us -> 6.63 us  [merge(): call(merge_kernel, 'merge', [shape(*gate.shape)] * 3 + [shape(1, units, d...]
    pallas_call x5 -> x4, Pallas kernels: 2.59 us -> 1.37 us  [the longest x1 1.05 us: finish(): call(finish_kernel, 'finish', [shape(rows // 2, features)] * 2 + [small]...]
  transfers between devices with their start and end apart: 32 -> 32, of which waited for: 13 -> 14; matrix products, arithmetic and copies ran while one was open for 2% -> 0% of each run, Pallas kernels for 22% -> 21%
where the time goes in v1:
time: 98.9 us; the launch traced here: 98.7 us
  starting transfers between devices  44.8 us (45%)
  waiting for transfers between devices  26.1 us (26%)
  Pallas kernels  25.6 us (26%)
  between operations  1.14 us (1%)
    ppermute x32, starting transfers between devices, swap(): return lax.ppermute(value, axis, [(i, i ^ distance) for i in range(size)])  44.8 us
    ppermute x32, waiting for transfers between devices, swap(): return lax.ppermute(value, axis, [(i, i ^ distance) for i in range(size)])  26.1 us
    pallas_call x1, Pallas kernels, merge(): call(merge_kernel, 'merge', [shape(*gate.shape)] * 3 + [shape(1, units, d...  6.63 us
    pallas_call x1, Pallas kernels, forward(): call(forward_kernel, 'forward', [shape(half, features)] * 2 + [shape(2 *...  5.45 us
    pallas_call x1, Pallas kernels, down_squares(): call(down_squares_kernel, 'down_squares', shape(1, weight.shape[1], dtype...  4.2 us
    pallas_call x1, Pallas kernels, backward(): call(backward_kernel, 'backward', [shape(2 * half, units)] * 2 + [shape(4...  4.09 us
    pallas_call x1, Pallas kernels, input_gradient_of(): call(input_gradient_kernel, 'input_gradient', [shape(rows, gate.shape[1])...  3.29 us
  transfers between devices with their start and end apart: 32, of which 14 were waited for; matrix products, arithmetic and copies ran while one was open for 0% of the time, Pallas kernels for 21%

profile of v1, /device:TPU:32, one launch (start us, length us, event | category | flops | bytes accessed | tf_op | source)
XLA Modules:
  0.0 98.7 jit_solution(2505340070954036352)
XLA Ops:
  0.8 5.5 %collective-permute-start = (bf16[16,2560]{1,0:T(8,128)(2,1)}, bf16[16,2560]{1,0:T(8,128)(2,1)S(1)}, u32[]{:S(2)}, u32[]{:S(2)}) collective-permute-start(bf16[16,2560]{1,0:T(8,128)(2,1)} %param.14), channel_id=1, source_target_pairs={{0,40},{8,32},{16,56},{24,48},{32,8},{40,0},{48,24},{56,16},{1,41}... | collective-permute-start | bytes 245768 | tf_op jit(solution)/shard_map/ppermute | solution.py:28
  6.2 4.2 %down_squares.1.value = f32[1,2560]{1,0:T(1,128)} custom-call(bf16[800,2560]{1,0:T(8,128)(2,1)} %w_ref.1, bf16[32,800]{1,0:T(8,128)(2,1)} %bitcast.16, bf16[32,2560]{1,0:T(8,128)(2,1)} %b_down.1), custom_call_target="tpu_custom_call" | custom-call | flops 1000 | bytes 1000 | tf_op jit(solution)/shard_map/down_squares/pallas_call | solution.py:105
  10.7 0.7 copy-done.6
  11.5 1.1 %collective-permute-done.4 = f32[1,2560]{1,0:T(1,128)S(1)} collective-permute-done((f32[1,2560]{1,0:T(1,128)S(1)}, f32[1,2560]{1,0:T(1,128)S(1)}, u32[]{:S(2)}, u32[]{:S(2)}) %collective-permute-start.4) | collective-permute-done | bytes 10272 | tf_op jit(solution)/shard_map/ppermute | solution.py:28
  12.6 2.4 %collective-permute-start.5 = (bf16[18,2560]{1,0:T(8,128)(2,1)S(1)}, bf16[18,2560]{1,0:T(8,128)(2,1)S(1)}, u32[]{:S(2)}, u32[]{:S(2)}) collective-permute-start(bf16[18,2560]{1,0:T(8,128)(2,1)S(1)} %pad_maximum_fusion.2), channel_id=1, source_target_pairs={{0,40},{8,32},{16,56},{24,48},{32,8},{40,0},{48,24},{56,16},{1,41}... | collective-permute-start | bytes 276488 | tf_op jit(solution)/shard_map/ppermute | solution.py:28
  15.1 1.6 %collective-permute-start.1 = (bf16[32,2560]{1,0:T(8,128)(2,1)S(1)}, bf16[32,2560]{1,0:T(8,128)(2,1)S(1)}, u32[]{:S(2)}, u32[]{:S(2)}) collective-permute-start(bf16[32,2560]{1,0:T(8,128)(2,1)S(1)} %get-tuple-element.113), channel_id=1, source_target_pairs={{0,2},{2,0},{4,6},{6,4},{1,3},{3,1},{5,7},{7,5},{8,10},{10,8},{12,... | collective-permute-start | bytes 491528 | tf_op jit(solution)/shard_map/ppermute | solution.py:28
  16.7 2.1 %collective-permute-start.2 = (bf16[32,2560]{1,0:T(8,128)(2,1)S(1)}, bf16[32,2560]{1,0:T(8,128)(2,1)S(1)}, u32[]{:S(2)}, u32[]{:S(2)}) collective-permute-start(bf16[32,2560]{1,0:T(8,128)(2,1)S(1)} %get-tuple-element.113), channel_id=1, source_target_pairs={{0,6},{2,4},{4,2},{6,0},{1,7},{3,5},{5,3},{7,1},{8,14},{10,12},{12... | collective-permute-start | bytes 491528 | tf_op jit(solution)/shard_map/ppermute | solution.py:28
  18.8 0.6 collective-permute-start.3
  19.4 3.5 %collective-permute-done.5 = bf16[18,2560]{1,0:T(8,128)(2,1)S(1)} collective-permute-done((bf16[18,2560]{1,0:T(8,128)(2,1)S(1)}, bf16[18,2560]{1,0:T(8,128)(2,1)S(1)}, u32[]{:S(2)}, u32[]{:S(2)}) %collective-permute-start.5) | collective-permute-done | bytes 92192 | tf_op jit(solution)/shard_map/ppermute | solution.py:28
  22.9 1.6 %collective-permute-start.6 = (bf16[34,2560]{1,0:T(8,128)(2,1)S(1)}, bf16[34,2560]{1,0:T(8,128)(2,1)S(1)}, u32[]{:S(2)}, u32[]{:S(2)}) collective-permute-start(bf16[34,2560]{1,0:T(8,128)(2,1)S(1)} %pad_maximum_fusion), channel_id=1, source_target_pairs={{0,2},{2,0},{4,6},{6,4},{1,3},{3,1},{5,7},{7,5},{8,10},{10,8},{12,... | collective-permute-start | bytes 522248 | tf_op jit(solution)/shard_map/ppermute | solution.py:28
  24.5 2.1 %collective-permute-start.7 = (bf16[34,2560]{1,0:T(8,128)(2,1)S(1)}, bf16[34,2560]{1,0:T(8,128)(2,1)S(1)}, u32[]{:S(2)}, u32[]{:S(2)}) collective-permute-start(bf16[34,2560]{1,0:T(8,128)(2,1)S(1)} %pad_maximum_fusion), channel_id=1, source_target_pairs={{0,6},{2,4},{4,2},{6,0},{1,7},{3,5},{5,3},{7,1},{8,14},{10,12},{12... | collective-permute-start | bytes 522248 | tf_op jit(solution)/shard_map/ppermute | solution.py:28
  26.6 0.7 collective-permute-start.8
  27.4 0.3 collective-permute-start.9
  27.8 6.6 %merge.1 = (bf16[800,2560]{1,0:T(8,128)(2,1)S(1)}, bf16[800,2560]{1,0:T(8,128)(2,1)S(1)}, bf16[800,2560]{1,0:T(8,128)(2,1)S(1)}, f32[1,800]{1,0:T(1,128)S(1)}, f32[1,800]{1,0:T(1,128)S(1)}) custom-call(bf16[128,2560]{1,0:T(8,128)(2,1)S(1)} %constant_dynamic-update-slice_fusion.2.after.mine, bf16[800,2560]{1,0:T(8,128)(2,1)} %bitcast.19, ...), custom_call_target="tpu_custom_call" | custom-call | flops 1000 | bytes 1000 | tf_op jit(solution)/shard_map/merge/pallas_call | solution.py:150
  34.4 2.0 %collective-permute-done.7.b = bf16[34,2560]{1,0:T(8,128)(2,1)S(1)} collective-permute-done((bf16[34,2560]{1,0:T(8,128)(2,1)S(1)}, bf16[34,2560]{1,0:T(8,128)(2,1)S(1)}, u32[]{:S(2)}, u32[]{:S(2)}) %collective-permute-start.7) | collective-permute-done | bytes 174112 | tf_op jit(solution)/shard_map/ppermute | solution.py:28
  36.5 0.3 collective-permute-start.11
  36.9 5.4 %forward.1 = (bf16[128,2560]{1,0:T(8,128)(2,1)S(1)}, bf16[128,2560]{1,0:T(8,128)(2,1)S(1)}, bf16[256,800]{1,0:T(8,128)(2,1)S(1)}, bf16[256,800]{1,0:T(8,128)(2,1...) custom-call(bf16[128,2560]{1,0:T(8,128)(2,1)S(1)} %join_cot.1.after.cot_mine, ...), custom_call_target="tpu_custom_call" | custom-call | flops 1000 | bytes 1000 | tf_op jit(solution)/shard_map/forward/pallas_call | solution.py:190
  42.3 4.1 %backward.1 = (bf16[256,800]{1,0:T(8,128)(2,1)S(1)}, bf16[256,800]{1,0:T(8,128)(2,1)S(1)}, bf16[4,64,640]{2,1,0:T(8,128)(2,1)S(1)}, bf16[4,64,640]{2,1,0:T(8,128)(2,1)S(1)}, bf16[4,48,640]{2,1,0:T(8,128)(2,1)S(1)}) custom-call(s32[1]{0:T(128)} %bitcast.y, s32[1]{0:T(128)} %bitcast.2.core, bf16[128,2560]{1,0:T(8,128)(2,1)S(1)} %join_cot.1.after.cot_mine, ...), custom_call_target="tpu_custom_call" | custom-call | flops 1000 | bytes 1000 | tf_op jit(solution)/shard_map/backward/pallas_call | solution.py:269
  46.4 0.6 collective-permute-start.12
  47.1 3.3 %input_gradient.1 = (bf16[128,2560]{1,0:T(8,128)(2,1)S(1)}, bf16[128,2560]{1,0:T(8,128)(2,1)S(1)}) custom-call(bf16[256,800]{1,0:T(8,128)(2,1)S(1)} %get-tuple-element.72.delta_gate, bf16[256,800]{1,0:T(8,128)(2,1)S(1)} %get-tuple-element.73.delta_up, bf16[800,2560]{1,0:T(8,128)(2,1)S(1)} %get-tuple-element.61.gate, bf16[800,2560]{1,0:T(8,128)(2,1)S(1)} %get-tuple-element.62.up), custom_call_target="tpu_custom_call" | custom-call | flops 2097152000 | bytes 1000 | tf_op jit(solution)/shard_map/input_gradient/pallas_call | solution.py:291
  50.5 0.5 collective-permute-start.13
  51.0 1.6 %collective-permute-start.18 = (bf16[96,640]{1,0:T(8,128)(2,1)S(1)}, bf16[96,640]{1,0:T(8,128)(2,1)S(1)}, u32[]{:S(2)}, u32[]{:S(2)}) collective-permute-start(bf16[96,640]{1,0:T(8,128)(2,1)S(1)} %get-tuple-element.87), channel_id=1, source_target_pairs={{0,64},{64,0},{128,192},{192,128},{1,65},{65,1},{129,193},{193,129... | collective-permute-start | bytes 368648 | tf_op jit(solution)/shard_map/ppermute | solution.py:28
  52.6 2.9 %collective-permute-start.19 = (bf16[96,640]{1,0:T(8,128)(2,1)S(1)}, bf16[96,640]{1,0:T(8,128)(2,1)S(1)}, u32[]{:S(2)}, u32[]{:S(2)}) collective-permute-start(bf16[96,640]{1,0:T(8,128)(2,1)S(1)} %get-tuple-element.88), channel_id=1, source_target_pairs={{0,128},{64,192},{128,0},{192,64},{1,129},{65,193},{129,1},{193,65... | collective-permute-start | bytes 368648 | tf_op jit(solution)/shard_map/ppermute | solution.py:28
  55.5 0.2 collective-permute-start.20
  55.7 0.3 half_sum.1
  56.1 2.2 %collective-permute-start.15 = (bf16[64,2560]{1,0:T(8,128)(2,1)S(1)}, bf16[64,2560]{1,0:T(8,128)(2,1)S(1)}, u32[]{:S(2)}, u32[]{:S(2)}) collective-permute-start(bf16[64,2560]{1,0:T(8,128)(2,1)S(1)} %get-tuple-element.82), channel_id=1, source_target_pairs={{0,6},{2,4},{4,2},{6,0},{1,7},{3,5},{5,3},{7,1},{8,14},{10,12},{12... | collective-permute-start | bytes 983048 | tf_op jit(solution)/shard_map/ppermute | solution.py:28
  58.3 1.9 %collective-permute-start.16 = (bf16[64,2560]{1,0:T(8,128)(2,1)S(1)}, bf16[64,2560]{1,0:T(8,128)(2,1)S(1)}, u32[]{:S(2)}, u32[]{:S(2)}) collective-permute-start(bf16[64,2560]{1,0:T(8,128)(2,1)S(1)} %get-tuple-element.83), channel_id=1, source_target_pairs={{0,4},{2,6},{4,0},{6,2},{1,5},{3,7},{5,1},{7,3},{8,12},{10,14},{12... | collective-permute-start | bytes 983048 | tf_op jit(solution)/shard_map/ppermute | solution.py:28
  60.2 1.3 %collective-permute-done.19.b = bf16[96,640]{1,0:T(8,128)(2,1)S(1)} collective-permute-done((bf16[96,640]{1,0:T(8,128)(2,1)S(1)}, bf16[96,640]{1,0:T(8,128)(2,1)S(1)}, u32[]{:S(2)}, u32[]{:S(2)}) %collective-permute-start.19) | collective-permute-done | bytes 122912 | tf_op jit(solution)/shard_map/ppermute | solution.py:28
  61.6 2.1 %collective-permute-done.20.c = bf16[96,640]{1,0:T(8,128)(2,1)S(1)} collective-permute-done((bf16[96,640]{1,0:T(8,128)(2,1)S(1)}, bf16[96,640]{1,0:T(8,128)(2,1)S(1)}, u32[]{:S(2)}, u32[]{:S(2)}) %collective-permute-start.20) | collective-permute-done | bytes 122912 | tf_op jit(solution)/shard_map/ppermute | solution.py:28
  63.9 2.0 %collective-permute-start.21 = (bf16[160,256]{1,0:T(8,128)(2,1)S(1)}, bf16[160,256]{1,0:T(8,128)(2,1)S(1)}, u32[]{:S(2)}, u32[]{:S(2)}) collective-permute-start(bf16[160,256]{1,0:T(8,128)(2,1)S(1)} %get-tuple-element.91), channel_id=1, source_target_pairs={{0,16},{16,0},{32,48},{48,32},{1,17},{17,1},{33,49},{49,33},{2,18}... | collective-permute-start | bytes 245768 | tf_op jit(solution)/shard_map/ppermute | solution.py:28
  65.9 0.5 collective-permute-start.22
  66.4 0.3 collective-permute-done.14.a
  66.8 1.0 %collective-permute-start.23 = (bf16[160,256]{1,0:T(8,128)(2,1)S(1)}, bf16[160,256]{1,0:T(8,128)(2,1)S(1)}, u32[]{:S(2)}, u32[]{:S(2)}) collective-permute-start(bf16[160,256]{1,0:T(8,128)(2,1)S(1)} %get-tuple-element.93), channel_id=1, source_target_pairs={{0,48},{16,32},{32,16},{48,0},{1,49},{17,33},{33,17},{49,1},{2,50}... | collective-permute-start | bytes 245768 | tf_op jit(solution)/shard_map/ppermute | solution.py:28
  67.7 4.2 %collective-permute-done.15.b = bf16[64,2560]{1,0:T(8,128)(2,1)S(1)} collective-permute-done((bf16[64,2560]{1,0:T(8,128)(2,1)S(1)}, bf16[64,2560]{1,0:T(8,128)(2,1)S(1)}, u32[]{:S(2)}, u32[]{:S(2)}) %collective-permute-start.15) | collective-permute-done | bytes 327712 | tf_op jit(solution)/shard_map/ppermute | solution.py:28
  72.0 1.8 %collective-permute-done.16.c = bf16[64,2560]{1,0:T(8,128)(2,1)S(1)} collective-permute-done((bf16[64,2560]{1,0:T(8,128)(2,1)S(1)}, bf16[64,2560]{1,0:T(8,128)(2,1)S(1)}, u32[]{:S(2)}, u32[]{:S(2)}) %collective-permute-start.16) | collective-permute-done | bytes 327712 | tf_op jit(solution)/shard_map/ppermute | solution.py:28
  73.9 1.3 %collective-permute-start.17 = (bf16[32,2560]{1,0:T(8,128)(2,1)S(1)}, bf16[32,2560]{1,0:T(8,128)(2,1)S(1)}, u32[]{:S(2)}, u32[]{:S(2)}) collective-permute-start(bf16[32,2560]{1,0:T(8,128)(2,1)S(1)} %get-tuple-element.85), channel_id=1, source_target_pairs={{0,40},{8,32},{16,56},{24,48},{32,8},{40,0},{48,24},{56,16},{1,41}... | collective-permute-start | bytes 491528 | tf_op jit(solution)/shard_map/ppermute | solution.py:28
  75.3 0.3 collective-permute-start.24
  75.6 2.1 %collective-permute-start.25 = (bf16[64,160]{1,0:T(8,128)(2,1)S(1)}, bf16[64,160]{1,0:T(8,128)(2,1)S(1)}, u32[]{:S(2)}, u32[]{:S(2)}) collective-permute-start(bf16[64,160]{1,0:T(8,128)(2,1)S(1)} %convert_element_type.62), channel_id=1, source_target_pairs={{0,6},{2,4},{4,2},{6,0},{1,7},{3,5},{5,3},{7,1},{8,14},{10,12},{12... | collective-permute-start | bytes 61448 | tf_op jit(solution)/shard_map/ppermute | solution.py:28
  77.7 1.8 %collective-permute-start.26 = (bf16[64,160]{1,0:T(8,128)(2,1)S(1)}, bf16[64,160]{1,0:T(8,128)(2,1)S(1)}, u32[]{:S(2)}, u32[]{:S(2)}) collective-permute-start(bf16[64,160]{1,0:T(8,128)(2,1)S(1)} %convert_element_type.62), channel_id=1, source_target_pairs={{0,4},{2,6},{4,0},{6,2},{1,5},{3,7},{5,1},{7,3},{8,12},{10,14},{12... | collective-permute-start | bytes 61448 | tf_op jit(solution)/shard_map/ppermute | solution.py:28
  79.5 1.3 %collective-permute-done.25.b = bf16[64,160]{1,0:T(8,128)(2,1)S(1)} collective-permute-done((bf16[64,160]{1,0:T(8,128)(2,1)S(1)}, bf16[64,160]{1,0:T(8,128)(2,1)S(1)}, u32[]{:S(2)}, u32[]{:S(2)}) %collective-permute-start.25) | collective-permute-done | bytes 20512 | tf_op jit(solution)/shard_map/ppermute | solution.py:28
  80.7 2.4 %collective-permute-done.26.c = bf16[64,160]{1,0:T(8,128)(2,1)S(1)} collective-permute-done((bf16[64,160]{1,0:T(8,128)(2,1)S(1)}, bf16[64,160]{1,0:T(8,128)(2,1)S(1)}, u32[]{:S(2)}, u32[]{:S(2)}) %collective-permute-start.26) | collective-permute-done | bytes 20512 | tf_op jit(solution)/shard_map/ppermute | solution.py:28
  83.1 1.1 %collective-permute-done.17.after.row_got = bf16[32,2560]{1,0:T(8,128)(2,1)S(1)} collective-permute-done((bf16[32,2560]{1,0:T(8,128)(2,1)S(1)}, bf16[32,2560]{1,0:T(8,128)(2,1)S(1)}, u32[]{:S(2)}, u32[]{:S(2)}) %collective-permute-start.17) | collective-permute-done | bytes 163872 | tf_op jit(solution)/shard_map/ppermute | solution.py:28
  84.3 3.7 %collective-permute-start.27 = (bf16[64,160]{1,0:T(8,128)(2,1)S(1)}, bf16[64,160]{1,0:T(8,128)(2,1)S(1)}, u32[]{:S(2)}, u32[]{:S(2)}) collective-permute-start(bf16[64,160]{1,0:T(8,128)(2,1)S(1)} %get-tuple-element.96), channel_id=1, source_target_pairs={{0,8},{8,0},{1,9},{9,1},{2,10},{10,2},{3,11},{11,3},{4,12},{12,4},... | collective-permute-start | bytes 61448 | tf_op jit(solution)/shard_map/ppermute | solution.py:28
  88.1 4.1 %collective-permute-start.30 = (bf16[32,800]{1,0:T(8,128)(2,1)S(1)}, bf16[32,800]{1,0:T(8,128)(2,1)S(1)}, u32[]{:S(2)}, u32[]{:S(2)}) collective-permute-start(bf16[32,800]{1,0:T(8,128)(2,1)S(1)} %get-tuple-element.97.own), channel_id=1, source_target_pairs={{0,128},{64,192},{128,0},{192,64},{1,129},{65,193},{129,1},{193,65... | collective-permute-start | bytes 153608 | tf_op jit(solution)/shard_map/ppermute | solution.py:28
  92.3 0.4 collective-permute-start.31
  92.8 2.2 %collective-permute-done.30.b = bf16[32,800]{1,0:T(8,128)(2,1)S(1)} collective-permute-done((bf16[32,800]{1,0:T(8,128)(2,1)S(1)}, bf16[32,800]{1,0:T(8,128)(2,1)S(1)}, u32[]{:S(2)}, u32[]{:S(2)}) %collective-permute-start.30) | collective-permute-done | bytes 51232 | tf_op jit(solution)/shard_map/ppermute | solution.py:28
  95.0 2.6 %collective-permute-done.31.c = bf16[32,800]{1,0:T(8,128)(2,1)S(1)} collective-permute-done((bf16[32,800]{1,0:T(8,128)(2,1)S(1)}, bf16[32,800]{1,0:T(8,128)(2,1)S(1)}, u32[]{:S(2)}, u32[]{:S(2)}) %collective-permute-start.31) | collective-permute-done | bytes 51232 | tf_op jit(solution)/shard_map/ppermute | solution.py:28
  97.7 1.1 %finish.1 = (bf16[16,2560]{1,0:T(8,128)(2,1)}, bf16[16,2560]{1,0:T(8,128)(2,1)}, f32[10,32]{1,0:T(8,128)}, f32[10,32]{1,0:T(8,128)}, f32[32,800]{1,0:T(8,128)}, ...) custom-call(s32[1]{0:T(128)} %bitcast.y, ...), custom_call_target="tpu_custom_call" | custom-call | flops 1000 | bytes 1000 | tf_op jit(solution)/shard_map/finish/pallas_call | solution.py:484
  (73 shorter events, 1.6 us)
Async XLA Ops:
  0.6 10.7 %copy-start.8 = (bf16[16,2560]{1,0:T(8,128)(2,1)S(1)}, bf16[16,2560]{1,0:T(8,128)(2,1)}, u32[]{:S(2)}) copy-start(bf16[16,2560]{1,0:T(8,128)(2,1)} %param.14) | copy-start | bytes 245764
  0.7 27.1 %copy-start.3 = (bf16[800,32]{0,1:T(8,128)(2,1)S(1)}, bf16[800,32]{0,1:T(8,128)(2,1)}, u32[]{:S(2)}) copy-start(bf16[800,32]{0,1:T(8,128)(2,1)} %param.22) | copy-start | bytes 153604
  0.7 27.1 %copy-start = (bf16[32,2560]{1,0:T(8,128)(2,1)S(1)}, bf16[32,2560]{1,0:T(8,128)(2,1)}, u32[]{:S(2)}) copy-start(bf16[32,2560]{1,0:T(8,128)(2,1)} %b_down.1) | copy-start | bytes 491524
  0.7 10.7 %copy-start.10 = (f32[800]{0:T(1024)S(1)}, f32[800]{0:T(1024)}, u32[]{:S(2)}) copy-start(f32[800]{0:T(1024)} %param.24) | copy-start | bytes 9604
  0.7 10.7 %copy-start.11 = (f32[800]{0:T(1024)S(1)}, f32[800]{0:T(1024)}, u32[]{:S(2)}) copy-start(f32[800]{0:T(1024)} %param.25) | copy-start | bytes 9604
  0.7 10.7 %copy-start.9 = (f32[2560]{0:T(1024)S(1)}, f32[2560]{0:T(1024)}, u32[]{:S(2)}) copy-start(f32[2560]{0:T(1024)} %param.26) | copy-start | bytes 30724
  0.7 11.9 %copy-start.7 = (bf16[16,2560]{1,0:T(8,128)(2,1)S(1)}, bf16[16,2560]{1,0:T(8,128)(2,1)}, u32[]{:S(2)}) copy-start(bf16[16,2560]{1,0:T(8,128)(2,1)} %param.27) | copy-start | bytes 245764
  0.7 27.0 %copy-start.1 = (bf16[2560,32]{0,1:T(8,128)(2,1)S(1)}, bf16[2560,32]{0,1:T(8,128)(2,1)}, u32[]{:S(2)}) copy-start(bf16[2560,32]{0,1:T(8,128)(2,1)} %param.18) | copy-start | bytes 491524
  0.7 27.0 %copy-start.2 = (bf16[2560,32]{0,1:T(8,128)(2,1)S(1)}, bf16[2560,32]{0,1:T(8,128)(2,1)}, u32[]{:S(2)}) copy-start(bf16[2560,32]{0,1:T(8,128)(2,1)} %param.20) | copy-start | bytes 491524
  0.7 27.0 %copy-start.4 = (bf16[32,800]{1,0:T(8,128)(2,1)S(1)}, bf16[32,800]{1,0:T(8,128)(2,1)}, u32[]{:S(2)}) copy-start(bf16[32,800]{1,0:T(8,128)(2,1)} %b_gate.1) | copy-start | bytes 153604
  0.7 27.0 %copy-start.5 = (bf16[32,800]{1,0:T(8,128)(2,1)S(1)}, bf16[32,800]{1,0:T(8,128)(2,1)}, u32[]{:S(2)}) copy-start(bf16[32,800]{1,0:T(8,128)(2,1)} %b_up.1) | copy-start | bytes 153604
  0.8 9.9 %collective-permute-start = (bf16[16,2560]{1,0:T(8,128)(2,1)}, bf16[16,2560]{1,0:T(8,128)(2,1)S(1)}, u32[]{:S(2)}, u32[]{:S(2)}) collective-permute-start(bf16[16,2560]{1,0:T(8,128)(2,1)} %param.14), channel_id=1, source_target_pairs={{0,40},{8,32},{16,56},{24,48},{32,8},{40,0},{48,24},{56,16},{1,41}... | collective-permute-start | bytes 245768 | tf_op jit(solution)/shard_map/ppermute | solution.py:28
  10.7 0.7 copy-start.6
  11.4 1.2 %collective-permute-start.4 = (f32[1,2560]{1,0:T(1,128)S(1)}, f32[1,2560]{1,0:T(1,128)S(1)}, u32[]{:S(2)}, u32[]{:S(2)}) collective-permute-start(f32[1,2560]{1,0:T(1,128)S(1)} %held_until.1), channel_id=1, source_target_pairs={{0,1},{1,0},{2,3},{3,2},{4,5},{5,4},{6,7},{7,6},{8,9},{9,8},{10,11... | collective-permute-start | bytes 30728 | tf_op jit(solution)/shard_map/ppermute | solution.py:28
  12.6 10.2 %collective-permute-start.5 = (bf16[18,2560]{1,0:T(8,128)(2,1)S(1)}, bf16[18,2560]{1,0:T(8,128)(2,1)S(1)}, u32[]{:S(2)}, u32[]{:S(2)}) collective-permute-start(bf16[18,2560]{1,0:T(8,128)(2,1)S(1)} %pad_maximum_fusion.2), channel_id=1, source_target_pairs={{0,40},{8,32},{16,56},{24,48},{32,8},{40,0},{48,24},{56,16},{1,41}... | collective-permute-start | bytes 276488 | tf_op jit(solution)/shard_map/ppermute | solution.py:28
  15.1 11.6 %collective-permute-start.1 = (bf16[32,2560]{1,0:T(8,128)(2,1)S(1)}, bf16[32,2560]{1,0:T(8,128)(2,1)S(1)}, u32[]{:S(2)}, u32[]{:S(2)}) collective-permute-start(bf16[32,2560]{1,0:T(8,128)(2,1)S(1)} %get-tuple-element.113), channel_id=1, source_target_pairs={{0,2},{2,0},{4,6},{6,4},{1,3},{3,1},{5,7},{7,5},{8,10},{10,8},{12,... | collective-permute-start | bytes 491528 | tf_op jit(solution)/shard_map/ppermute | solution.py:28
  16.7 10.7 %collective-permute-start.2 = (bf16[32,2560]{1,0:T(8,128)(2,1)S(1)}, bf16[32,2560]{1,0:T(8,128)(2,1)S(1)}, u32[]{:S(2)}, u32[]{:S(2)}) collective-permute-start(bf16[32,2560]{1,0:T(8,128)(2,1)S(1)} %get-tuple-element.113), channel_id=1, source_target_pairs={{0,6},{2,4},{4,2},{6,0},{1,7},{3,5},{5,3},{7,1},{8,14},{10,12},{12... | collective-permute-start | bytes 491528 | tf_op jit(solution)/shard_map/ppermute | solution.py:28
  18.8 8.7 %collective-permute-start.3 = (bf16[32,2560]{1,0:T(8,128)(2,1)S(1)}, bf16[32,2560]{1,0:T(8,128)(2,1)S(1)}, u32[]{:S(2)}, u32[]{:S(2)}) collective-permute-start(bf16[32,2560]{1,0:T(8,128)(2,1)S(1)} %get-tuple-element.113), channel_id=1, source_target_pairs={{0,4},{2,6},{4,0},{6,2},{1,5},{3,7},{5,1},{7,3},{8,12},{10,14},{12... | collective-permute-start | bytes 491528 | tf_op jit(solution)/shard_map/ppermute | solution.py:28
  22.9 11.5 %collective-permute-start.6 = (bf16[34,2560]{1,0:T(8,128)(2,1)S(1)}, bf16[34,2560]{1,0:T(8,128)(2,1)S(1)}, u32[]{:S(2)}, u32[]{:S(2)}) collective-permute-start(bf16[34,2560]{1,0:T(8,128)(2,1)S(1)} %pad_maximum_fusion), channel_id=1, source_target_pairs={{0,2},{2,0},{4,6},{6,4},{1,3},{3,1},{5,7},{7,5},{8,10},{10,8},{12,... | collective-permute-start | bytes 522248 | tf_op jit(solution)/shard_map/ppermute | solution.py:28
  24.5 11.9 %collective-permute-start.7 = (bf16[34,2560]{1,0:T(8,128)(2,1)S(1)}, bf16[34,2560]{1,0:T(8,128)(2,1)S(1)}, u32[]{:S(2)}, u32[]{:S(2)}) collective-permute-start(bf16[34,2560]{1,0:T(8,128)(2,1)S(1)} %pad_maximum_fusion), channel_id=1, source_target_pairs={{0,6},{2,4},{4,2},{6,0},{1,7},{3,5},{5,3},{7,1},{8,14},{10,12},{12... | collective-permute-start | bytes 522248 | tf_op jit(solution)/shard_map/ppermute | solution.py:28
  26.6 9.8 %collective-permute-start.8 = (bf16[34,2560]{1,0:T(8,128)(2,1)S(1)}, bf16[34,2560]{1,0:T(8,128)(2,1)S(1)}, u32[]{:S(2)}, u32[]{:S(2)}) collective-permute-start(bf16[34,2560]{1,0:T(8,128)(2,1)S(1)} %pad_maximum_fusion), channel_id=1, source_target_pairs={{0,4},{2,6},{4,0},{6,2},{1,5},{3,7},{5,1},{7,3},{8,12},{10,14},{12... | collective-permute-start | bytes 522248 | tf_op jit(solution)/shard_map/ppermute | solution.py:28
  27.4 9.4 %collective-permute-start.9 = (bf16[128,2560]{1,0:T(8,128)(2,1)S(1)}, bf16[128,2560]{1,0:T(8,128)(2,1)S(1)}, u32[]{:S(2)}, u32[]{:S(2)}) collective-permute-start(bf16[128,2560]{1,0:T(8,128)(2,1)S(1)} %constant_dynamic-update-slice_fusion.2.after.mine), channel_id=1, source_target_pairs={{0,1},{1,0},{2,3},{3,2},{4,5},{5,4},{6,7},{7,6},{8,9},{9,8},{10,11... | collective-permute-start | bytes 1966088 | tf_op jit(solution)/shard_map/ppermute | solution.py:28
  36.5 5.8 %collective-permute-start.11 = (bf16[128,2560]{1,0:T(8,128)(2,1)S(1)}, bf16[128,2560]{1,0:T(8,128)(2,1)S(1)}, u32[]{:S(2)}, u32[]{:S(2)}) collective-permute-start(bf16[128,2560]{1,0:T(8,128)(2,1)S(1)} %join_cot.1.after.cot_mine), channel_id=1, source_target_pairs={{0,1},{1,0},{2,3},{3,2},{4,5},{5,4},{6,7},{7,6},{8,9},{9,8},{10,11... | collective-permute-start | bytes 1966088 | tf_op jit(solution)/shard_map/ppermute | solution.py:28
  46.4 4.0 %collective-permute-start.12 = (bf16[4,64,640]{2,1,0:T(8,128)(2,1)S(1)}, bf16[4,64,640]{2,1,0:T(8,128)(2,1)S(1)}, u32[]{:S(2)}, u32[]{:S(2)}) collective-permute-start(bf16[4,64,640]{2,1,0:T(8,128)(2,1)S(1)} %get-tuple-element.77), channel_id=1, source_target_pairs={{0,1},{1,0},{2,3},{3,2},{4,5},{5,4},{6,7},{7,6},{8,9},{9,8},{10,11... | collective-permute-start | bytes 983048 | tf_op jit(solution)/shard_map/ppermute | solution.py:28
  47.0 8.7 %collective-permute-start.10 = (bf16[128,2560]{1,0:T(8,128)(2,1)S(1)}, bf16[128,2560]{1,0:T(8,128)(2,1)S(1)}, u32[]{:S(2)}, u32[]{:S(2)}) collective-permute-start(bf16[128,2560]{1,0:T(8,128)(2,1)S(1)} %get-tuple-element.66.p_away), channel_id=1, source_target_pairs={{0,1},{1,0},{2,3},{3,2},{4,5},{5,4},{6,7},{7,6},{8,9},{9,8},{10,11... | collective-permute-start | bytes 1966088 | tf_op jit(solution)/shard_map/ppermute | solution.py:28
  50.5 5.2 %collective-permute-start.13 = (bf16[128,2560]{1,0:T(8,128)(2,1)S(1)}, bf16[128,2560]{1,0:T(8,128)(2,1)S(1)}, u32[]{:S(2)}, u32[]{:S(2)}) collective-permute-start(bf16[128,2560]{1,0:T(8,128)(2,1)S(1)} %get-tuple-element.79), channel_id=1, source_target_pairs={{0,1},{1,0},{2,3},{3,2},{4,5},{5,4},{6,7},{7,6},{8,9},{9,8},{10,11... | collective-permute-start | bytes 1966088 | tf_op jit(solution)/shard_map/ppermute | solution.py:28
  51.0 7.3 %collective-permute-start.18 = (bf16[96,640]{1,0:T(8,128)(2,1)S(1)}, bf16[96,640]{1,0:T(8,128)(2,1)S(1)}, u32[]{:S(2)}, u32[]{:S(2)}) collective-permute-start(bf16[96,640]{1,0:T(8,128)(2,1)S(1)} %get-tuple-element.87), channel_id=1, source_target_pairs={{0,64},{64,0},{128,192},{192,128},{1,65},{65,1},{129,193},{193,129... | collective-permute-start | bytes 368648 | tf_op jit(solution)/shard_map/ppermute | solution.py:28
  52.6 8.9 %collective-permute-start.19 = (bf16[96,640]{1,0:T(8,128)(2,1)S(1)}, bf16[96,640]{1,0:T(8,128)(2,1)S(1)}, u32[]{:S(2)}, u32[]{:S(2)}) collective-permute-start(bf16[96,640]{1,0:T(8,128)(2,1)S(1)} %get-tuple-element.88), channel_id=1, source_target_pairs={{0,128},{64,192},{128,0},{192,64},{1,129},{65,193},{129,1},{193,65... | collective-permute-start | bytes 368648 | tf_op jit(solution)/shard_map/ppermute | solution.py:28
  55.5 8.2 %collective-permute-start.20 = (bf16[96,640]{1,0:T(8,128)(2,1)S(1)}, bf16[96,640]{1,0:T(8,128)(2,1)S(1)}, u32[]{:S(2)}, u32[]{:S(2)}) collective-permute-start(bf16[96,640]{1,0:T(8,128)(2,1)S(1)} %get-tuple-element.89), channel_id=1, source_target_pairs={{0,192},{64,128},{128,64},{192,0},{1,193},{65,129},{129,65},{193,1... | collective-permute-start | bytes 368648 | tf_op jit(solution)/shard_map/ppermute | solution.py:28
  56.0 10.7 %collective-permute-start.14 = (bf16[64,2560]{1,0:T(8,128)(2,1)S(1)}, bf16[64,2560]{1,0:T(8,128)(2,1)S(1)}, u32[]{:S(2)}, u32[]{:S(2)}) collective-permute-start(bf16[64,2560]{1,0:T(8,128)(2,1)S(1)} %get-tuple-element.81), channel_id=1, source_target_pairs={{0,2},{2,0},{4,6},{6,4},{1,3},{3,1},{5,7},{7,5},{8,10},{10,8},{12,... | collective-permute-start | bytes 983048 | tf_op jit(solution)/shard_map/ppermute | solution.py:28
  56.1 15.8 %collective-permute-start.15 = (bf16[64,2560]{1,0:T(8,128)(2,1)S(1)}, bf16[64,2560]{1,0:T(8,128)(2,1)S(1)}, u32[]{:S(2)}, u32[]{:S(2)}) collective-permute-start(bf16[64,2560]{1,0:T(8,128)(2,1)S(1)} %get-tuple-element.82), channel_id=1, source_target_pairs={{0,6},{2,4},{4,2},{6,0},{1,7},{3,5},{5,3},{7,1},{8,14},{10,12},{12... | collective-permute-start | bytes 983048 | tf_op jit(solution)/shard_map/ppermute | solution.py:28
  58.3 15.4 %collective-permute-start.16 = (bf16[64,2560]{1,0:T(8,128)(2,1)S(1)}, bf16[64,2560]{1,0:T(8,128)(2,1)S(1)}, u32[]{:S(2)}, u32[]{:S(2)}) collective-permute-start(bf16[64,2560]{1,0:T(8,128)(2,1)S(1)} %get-tuple-element.83), channel_id=1, source_target_pairs={{0,4},{2,6},{4,0},{6,2},{1,5},{3,7},{5,1},{7,3},{8,12},{10,14},{12... | collective-permute-start | bytes 983048 | tf_op jit(solution)/shard_map/ppermute | solution.py:28
  63.9 11.3 %collective-permute-start.21 = (bf16[160,256]{1,0:T(8,128)(2,1)S(1)}, bf16[160,256]{1,0:T(8,128)(2,1)S(1)}, u32[]{:S(2)}, u32[]{:S(2)}) collective-permute-start(bf16[160,256]{1,0:T(8,128)(2,1)S(1)} %get-tuple-element.91), channel_id=1, source_target_pairs={{0,16},{16,0},{32,48},{48,32},{1,17},{17,1},{33,49},{49,33},{2,18}... | collective-permute-start | bytes 245768 | tf_op jit(solution)/shard_map/ppermute | solution.py:28
  65.9 9.3 %collective-permute-start.22 = (bf16[160,256]{1,0:T(8,128)(2,1)S(1)}, bf16[160,256]{1,0:T(8,128)(2,1)S(1)}, u32[]{:S(2)}, u32[]{:S(2)}) collective-permute-start(bf16[160,256]{1,0:T(8,128)(2,1)S(1)} %get-tuple-element.92), channel_id=1, source_target_pairs={{0,32},{16,48},{32,0},{48,16},{1,33},{17,49},{33,1},{49,17},{2,34}... | collective-permute-start | bytes 245768 | tf_op jit(solution)/shard_map/ppermute | solution.py:28
  66.8 8.4 %collective-permute-start.23 = (bf16[160,256]{1,0:T(8,128)(2,1)S(1)}, bf16[160,256]{1,0:T(8,128)(2,1)S(1)}, u32[]{:S(2)}, u32[]{:S(2)}) collective-permute-start(bf16[160,256]{1,0:T(8,128)(2,1)S(1)} %get-tuple-element.93), channel_id=1, source_target_pairs={{0,48},{16,32},{32,16},{48,0},{1,49},{17,33},{33,17},{49,1},{2,50}... | collective-permute-start | bytes 245768 | tf_op jit(solution)/shard_map/ppermute | solution.py:28
  73.9 10.3 %collective-permute-start.17 = (bf16[32,2560]{1,0:T(8,128)(2,1)S(1)}, bf16[32,2560]{1,0:T(8,128)(2,1)S(1)}, u32[]{:S(2)}, u32[]{:S(2)}) collective-permute-start(bf16[32,2560]{1,0:T(8,128)(2,1)S(1)} %get-tuple-element.85), channel_id=1, source_target_pairs={{0,40},{8,32},{16,56},{24,48},{32,8},{40,0},{48,24},{56,16},{1,41}... | collective-permute-start | bytes 491528 | tf_op jit(solution)/shard_map/ppermute | solution.py:28
  75.3 4.2 %collective-permute-start.24 = (bf16[64,160]{1,0:T(8,128)(2,1)S(1)}, bf16[64,160]{1,0:T(8,128)(2,1)S(1)}, u32[]{:S(2)}, u32[]{:S(2)}) collective-permute-start(bf16[64,160]{1,0:T(8,128)(2,1)S(1)} %convert_element_type.62), channel_id=1, source_target_pairs={{0,2},{2,0},{4,6},{6,4},{1,3},{3,1},{5,7},{7,5},{8,10},{10,8},{12,... | collective-permute-start | bytes 61448 | tf_op jit(solution)/shard_map/ppermute | solution.py:28
  75.6 5.1 %collective-permute-start.25 = (bf16[64,160]{1,0:T(8,128)(2,1)S(1)}, bf16[64,160]{1,0:T(8,128)(2,1)S(1)}, u32[]{:S(2)}, u32[]{:S(2)}) collective-permute-start(bf16[64,160]{1,0:T(8,128)(2,1)S(1)} %convert_element_type.62), channel_id=1, source_target_pairs={{0,6},{2,4},{4,2},{6,0},{1,7},{3,5},{5,3},{7,1},{8,14},{10,12},{12... | collective-permute-start | bytes 61448 | tf_op jit(solution)/shard_map/ppermute | solution.py:28
  77.7 5.4 %collective-permute-start.26 = (bf16[64,160]{1,0:T(8,128)(2,1)S(1)}, bf16[64,160]{1,0:T(8,128)(2,1)S(1)}, u32[]{:S(2)}, u32[]{:S(2)}) collective-permute-start(bf16[64,160]{1,0:T(8,128)(2,1)S(1)} %convert_element_type.62), channel_id=1, source_target_pairs={{0,4},{2,6},{4,0},{6,2},{1,5},{3,7},{5,1},{7,3},{8,12},{10,14},{12... | collective-permute-start | bytes 61448 | tf_op jit(solution)/shard_map/ppermute | solution.py:28
  84.3 8.4 %collective-permute-start.27 = (bf16[64,160]{1,0:T(8,128)(2,1)S(1)}, bf16[64,160]{1,0:T(8,128)(2,1)S(1)}, u32[]{:S(2)}, u32[]{:S(2)}) collective-permute-start(bf16[64,160]{1,0:T(8,128)(2,1)S(1)} %get-tuple-element.96), channel_id=1, source_target_pairs={{0,8},{8,0},{1,9},{9,1},{2,10},{10,2},{3,11},{11,3},{4,12},{12,4},... | collective-permute-start | bytes 61448 | tf_op jit(solution)/shard_map/ppermute | solution.py:28
  88.0 4.8 %collective-permute-start.29 = (bf16[32,800]{1,0:T(8,128)(2,1)S(1)}, bf16[32,800]{1,0:T(8,128)(2,1)S(1)}, u32[]{:S(2)}, u32[]{:S(2)}) collective-permute-start(bf16[32,800]{1,0:T(8,128)(2,1)S(1)} %get-tuple-element.97.own), channel_id=1, source_target_pairs={{0,64},{64,0},{128,192},{192,128},{1,65},{65,1},{129,193},{193,129... | collective-permute-start | bytes 153608 | tf_op jit(solution)/shard_map/ppermute | solution.py:28
  88.1 6.9 %collective-permute-start.30 = (bf16[32,800]{1,0:T(8,128)(2,1)S(1)}, bf16[32,800]{1,0:T(8,128)(2,1)S(1)}, u32[]{:S(2)}, u32[]{:S(2)}) collective-permute-start(bf16[32,800]{1,0:T(8,128)(2,1)S(1)} %get-tuple-element.97.own), channel_id=1, source_target_pairs={{0,128},{64,192},{128,0},{192,64},{1,129},{65,193},{129,1},{193,65... | collective-permute-start | bytes 153608 | tf_op jit(solution)/shard_map/ppermute | solution.py:28
  92.3 5.4 %collective-permute-start.31 = (bf16[32,800]{1,0:T(8,128)(2,1)S(1)}, bf16[32,800]{1,0:T(8,128)(2,1)S(1)}, u32[]{:S(2)}, u32[]{:S(2)}) collective-permute-start(bf16[32,800]{1,0:T(8,128)(2,1)S(1)} %get-tuple-element.97.own), channel_id=1, source_target_pairs={{0,192},{64,128},{128,64},{192,0},{1,193},{65,129},{129,65},{193,1... | collective-permute-start | bytes 153608 | tf_op jit(solution)/shard_map/ppermute | solution.py:28
  92.7 5.0 %collective-permute-start.28 = (f32[64,160]{1,0:T(8,128)S(1)}, f32[64,160]{1,0:T(8,128)S(1)}, u32[]{:S(2)}, u32[]{:S(2)}) collective-permute-start(f32[64,160]{1,0:T(8,128)S(1)} %convert_add_fusion.shared), channel_id=1, source_target_pairs={{0,1},{1,0},{2,3},{3,2},{4,5},{5,4},{6,7},{7,6},{8,9},{9,8},{10,11... | collective-permute-start | bytes 122888 | tf_op jit(solution)/shard_map/ppermute | solution.py:28

commit v2 on v1

--- a/solution.py
+++ b/solution.py
@@ -14,6 +14,7 @@
 TENSOR = ("zh", "x", "c")
 ALL = DATA + TENSOR
 X_ORDER = (1, 3, 2)
+FAR_FIRST = (2, 1, 3)
 MIB = 1024 * 1024
 ANY = pl.BlockSpec(memory_space=pl.ANY)
 VMEM = pl.BlockSpec(memory_space=pltpu.VMEM)
@@ -576,15 +577,17 @@
     i_mine, i_away = input_gradient_of(delta_gate, delta_up, gate, up)
     i_away, *packed = core_sum(i_away, shared_own, swap_core(shared_away), local)
     pair, *sent = half_sum(p_mine, p_got, i_mine, swap_core(i_away))
-    own, *sent_z = after_y(zl, pair, packed[0], [swap(packed[k], "y", k, 4) for k in (1, 2, 3)])
+    own, *sent_z = after_y(zl, pair, packed[0], [swap(packed[k], "y", k, 4) for k in FAR_FIRST])
 
     row_own, sent = pair_sum(pair, [swap(v, "x", k, 4) for k, v in zip(X_ORDER, sent)])
     row_got = swap_z(sent)
 
     quarter = features // 16
-    shared, local = after_z(packed[0], own, [swap(v, "zl", k + 1, 4) for k, v in enumerate(sent_z)], quarter, units)
-    others = [swap(local, "y", k, 4) for k in (1, 2, 3)]
-    shared, sent_zh = x_sum(row_got, shared, swap_x(shared.astype(bf16)))
+    shared, local = after_z(packed[0], own, [swap(sent_z[k - 1], "zl", k, 4) for k in (1, 2, 3)], quarter, units)
+    shared_sent = shared.astype(bf16)
+    by_distance = {k: swap(local, "y", k, 4) for k in FAR_FIRST}
+    others = [by_distance[k] for k in (1, 2, 3)]
+    shared, sent_zh = x_sum(row_got, shared, [swap(shared_sent, "x", k, 4) for k in FAR_FIRST])
     shared = shared + swap(sent_zh, "zh", 1, 2).astype(f32)
     outputs, input_gradient, gate_in, up_in, gate_out, up_out, down_out, down_in, gate_m, up_m, down_m = finish(
         y, place[None], core, row_own, row_got, squares, m_down, shared, swap_core(shared), local, others

time: 98.9 us -> 98.4 us (level)
  transfers between devices with their start and end apart: 32 -> 32, of which waited for: 14 -> 16; matrix products, arithmetic and copies ran while one was open for 0% -> 0% of each run, Pallas kernels for 21% -> 21%
where the time goes in v2:
time: 98.4 us; the launch traced here: 98.2 us
  starting transfers between devices  44 us (45%)
  waiting for transfers between devices  26.4 us (27%)
  Pallas kernels  25.6 us (26%)
  between operations  1.14 us (1%)
    ppermute x32, starting transfers between devices, swap(): return lax.ppermute(value, axis, [(i, i ^ distance) for i in range(size)])  44 us
    ppermute x32, waiting for transfers between devices, swap(): return lax.ppermute(value, axis, [(i, i ^ distance) for i in range(size)])  26.4 us
    pallas_call x1, Pallas kernels, merge(): call(merge_kernel, 'merge', [shape(*gate.shape)] * 3 + [shape(1, units, d...  6.63 us
    pallas_call x1, Pallas kernels, forward(): call(forward_kernel, 'forward', [shape(half, features)] * 2 + [shape(2 *...  5.45 us
    pallas_call x1, Pallas kernels, down_squares(): call(down_squares_kernel, 'down_squares', shape(1, weight.shape[1], dtype...  4.2 us
    pallas_call x1, Pallas kernels, backward(): call(backward_kernel, 'backward', [shape(2 * half, units)] * 2 + [shape(4...  4.09 us
    pallas_call x1, Pallas kernels, input_gradient_of(): call(input_gradient_kernel, 'input_gradient', [shape(rows, gate.shape[1])...  3.29 us
  transfers between devices with their start and end apart: 32, of which 16 were waited for; matrix products, arithmetic and copies ran while one was open for 0% of the time, Pallas kernels for 21%

profile of v2, /device:TPU:32, one launch (start us, length us, event | category | flops | bytes accessed | tf_op | source)
XLA Modules:
  0.0 98.2 jit_solution(10087375007444490046)
XLA Ops:
  0.8 5.5 %collective-permute-start = (bf16[16,2560]{1,0:T(8,128)(2,1)}, bf16[16,2560]{1,0:T(8,128)(2,1)S(1)}, u32[]{:S(2)}, u32[]{:S(2)}) collective-permute-start(bf16[16,2560]{1,0:T(8,128)(2,1)} %param.14), channel_id=1, source_target_pairs={{0,40},{8,32},{16,56},{24,48},{32,8},{40,0},{48,24},{56,16},{1,41}... | collective-permute-start | bytes 245768 | tf_op jit(solution)/shard_map/ppermute | solution.py:29
  6.2 4.2 %down_squares.1.value = f32[1,2560]{1,0:T(1,128)} custom-call(bf16[800,2560]{1,0:T(8,128)(2,1)} %w_ref.1, bf16[32,800]{1,0:T(8,128)(2,1)} %bitcast.16, bf16[32,2560]{1,0:T(8,128)(2,1)} %b_down.1), custom_call_target="tpu_custom_call" | custom-call | flops 1000 | bytes 1000 | tf_op jit(solution)/shard_map/down_squares/pallas_call | solution.py:106
  10.7 0.7 copy-done.6
  11.5 1.1 %collective-permute-done.4 = f32[1,2560]{1,0:T(1,128)S(1)} collective-permute-done((f32[1,2560]{1,0:T(1,128)S(1)}, f32[1,2560]{1,0:T(1,128)S(1)}, u32[]{:S(2)}, u32[]{:S(2)}) %collective-permute-start.4) | collective-permute-done | bytes 10272 | tf_op jit(solution)/shard_map/ppermute | solution.py:29
  12.6 2.4 %collective-permute-start.5 = (bf16[18,2560]{1,0:T(8,128)(2,1)S(1)}, bf16[18,2560]{1,0:T(8,128)(2,1)S(1)}, u32[]{:S(2)}, u32[]{:S(2)}) collective-permute-start(bf16[18,2560]{1,0:T(8,128)(2,1)S(1)} %pad_maximum_fusion.2), channel_id=1, source_target_pairs={{0,40},{8,32},{16,56},{24,48},{32,8},{40,0},{48,24},{56,16},{1,41}... | collective-permute-start | bytes 276488 | tf_op jit(solution)/shard_map/ppermute | solution.py:29
  15.1 1.6 %collective-permute-start.1 = (bf16[32,2560]{1,0:T(8,128)(2,1)S(1)}, bf16[32,2560]{1,0:T(8,128)(2,1)S(1)}, u32[]{:S(2)}, u32[]{:S(2)}) collective-permute-start(bf16[32,2560]{1,0:T(8,128)(2,1)S(1)} %get-tuple-element.113), channel_id=1, source_target_pairs={{0,2},{2,0},{4,6},{6,4},{1,3},{3,1},{5,7},{7,5},{8,10},{10,8},{12,... | collective-permute-start | bytes 491528 | tf_op jit(solution)/shard_map/ppermute | solution.py:29
  16.7 2.1 %collective-permute-start.2 = (bf16[32,2560]{1,0:T(8,128)(2,1)S(1)}, bf16[32,2560]{1,0:T(8,128)(2,1)S(1)}, u32[]{:S(2)}, u32[]{:S(2)}) collective-permute-start(bf16[32,2560]{1,0:T(8,128)(2,1)S(1)} %get-tuple-element.113), channel_id=1, source_target_pairs={{0,6},{2,4},{4,2},{6,0},{1,7},{3,5},{5,3},{7,1},{8,14},{10,12},{12... | collective-permute-start | bytes 491528 | tf_op jit(solution)/shard_map/ppermute | solution.py:29
  18.8 0.6 collective-permute-start.3
  19.4 3.5 %collective-permute-done.5 = bf16[18,2560]{1,0:T(8,128)(2,1)S(1)} collective-permute-done((bf16[18,2560]{1,0:T(8,128)(2,1)S(1)}, bf16[18,2560]{1,0:T(8,128)(2,1)S(1)}, u32[]{:S(2)}, u32[]{:S(2)}) %collective-permute-start.5) | collective-permute-done | bytes 92192 | tf_op jit(solution)/shard_map/ppermute | solution.py:29
  22.9 1.6 %collective-permute-start.6 = (bf16[34,2560]{1,0:T(8,128)(2,1)S(1)}, bf16[34,2560]{1,0:T(8,128)(2,1)S(1)}, u32[]{:S(2)}, u32[]{:S(2)}) collective-permute-start(bf16[34,2560]{1,0:T(8,128)(2,1)S(1)} %pad_maximum_fusion), channel_id=1, source_target_pairs={{0,2},{2,0},{4,6},{6,4},{1,3},{3,1},{5,7},{7,5},{8,10},{10,8},{12,... | collective-permute-start | bytes 522248 | tf_op jit(solution)/shard_map/ppermute | solution.py:29
  24.5 2.1 %collective-permute-start.7 = (bf16[34,2560]{1,0:T(8,128)(2,1)S(1)}, bf16[34,2560]{1,0:T(8,128)(2,1)S(1)}, u32[]{:S(2)}, u32[]{:S(2)}) collective-permute-start(bf16[34,2560]{1,0:T(8,128)(2,1)S(1)} %pad_maximum_fusion), channel_id=1, source_target_pairs={{0,6},{2,4},{4,2},{6,0},{1,7},{3,5},{5,3},{7,1},{8,14},{10,12},{12... | collective-permute-start | bytes 522248 | tf_op jit(solution)/shard_map/ppermute | solution.py:29
  26.6 0.7 collective-permute-start.8
  27.8 6.6 %merge.1 = (bf16[800,2560]{1,0:T(8,128)(2,1)S(1)}, bf16[800,2560]{1,0:T(8,128)(2,1)S(1)}, bf16[800,2560]{1,0:T(8,128)(2,1)S(1)}, f32[1,800]{1,0:T(1,128)S(1)}, f32[1,800]{1,0:T(1,128)S(1)}) custom-call(bf16[128,2560]{1,0:T(8,128)(2,1)S(1)} %constant_dynamic-update-slice_fusion.2.after.mine, bf16[800,2560]{1,0:T(8,128)(2,1)} %bitcast.19, ...), custom_call_target="tpu_custom_call" | custom-call | flops 1000 | bytes 1000 | tf_op jit(solution)/shard_map/merge/pallas_call | solution.py:151
  34.4 2.0 %collective-permute-done.7.b = bf16[34,2560]{1,0:T(8,128)(2,1)S(1)} collective-permute-done((bf16[34,2560]{1,0:T(8,128)(2,1)S(1)}, bf16[34,2560]{1,0:T(8,128)(2,1)S(1)}, u32[]{:S(2)}, u32[]{:S(2)}) %collective-permute-start.7) | collective-permute-done | bytes 174112 | tf_op jit(solution)/shard_map/ppermute | solution.py:29
  36.5 0.3 collective-permute-start.11
  36.9 5.4 %forward.1 = (bf16[128,2560]{1,0:T(8,128)(2,1)S(1)}, bf16[128,2560]{1,0:T(8,128)(2,1)S(1)}, bf16[256,800]{1,0:T(8,128)(2,1)S(1)}, bf16[256,800]{1,0:T(8,128)(2,1...) custom-call(bf16[128,2560]{1,0:T(8,128)(2,1)S(1)} %join_cot.1.after.cot_mine, ...), custom_call_target="tpu_custom_call" | custom-call | flops 1000 | bytes 1000 | tf_op jit(solution)/shard_map/forward/pallas_call | solution.py:191
  42.3 4.1 %backward.1 = (bf16[256,800]{1,0:T(8,128)(2,1)S(1)}, bf16[256,800]{1,0:T(8,128)(2,1)S(1)}, bf16[4,64,640]{2,1,0:T(8,128)(2,1)S(1)}, bf16[4,64,640]{2,1,0:T(8,128)(2,1)S(1)}, bf16[4,48,640]{2,1,0:T(8,128)(2,1)S(1)}) custom-call(s32[1]{0:T(128)} %bitcast.y, s32[1]{0:T(128)} %bitcast.2.core, bf16[128,2560]{1,0:T(8,128)(2,1)S(1)} %join_cot.1.after.cot_mine, ...), custom_call_target="tpu_custom_call" | custom-call | flops 1000 | bytes 1000 | tf_op jit(solution)/shard_map/backward/pallas_call | solution.py:270
  46.4 0.6 collective-permute-start.12
  47.1 3.3 %input_gradient.1 = (bf16[128,2560]{1,0:T(8,128)(2,1)S(1)}, bf16[128,2560]{1,0:T(8,128)(2,1)S(1)}) custom-call(bf16[256,800]{1,0:T(8,128)(2,1)S(1)} %get-tuple-element.72.delta_gate, bf16[256,800]{1,0:T(8,128)(2,1)S(1)} %get-tuple-element.73.delta_up, bf16[800,2560]{1,0:T(8,128)(2,1)S(1)} %get-tuple-element.61.gate, bf16[800,2560]{1,0:T(8,128)(2,1)S(1)} %get-tuple-element.62.up), custom_call_target="tpu_custom_call" | custom-call | flops 2097152000 | bytes 1000 | tf_op jit(solution)/shard_map/input_gradient/pallas_call | solution.py:292
  50.5 0.5 collective-permute-start.13
  51.0 3.2 %collective-permute-start.18 = (bf16[96,640]{1,0:T(8,128)(2,1)S(1)}, bf16[96,640]{1,0:T(8,128)(2,1)S(1)}, u32[]{:S(2)}, u32[]{:S(2)}) collective-permute-start(bf16[96,640]{1,0:T(8,128)(2,1)S(1)} %get-tuple-element.87), channel_id=1, source_target_pairs={{0,128},{64,192},{128,0},{192,64},{1,129},{65,193},{129,1},{193,65... | collective-permute-start | bytes 368648 | tf_op jit(solution)/shard_map/ppermute | solution.py:29
  54.2 0.7 collective-permute-start.19
  54.9 0.4 collective-permute-start.20
  55.3 0.3 half_sum.1
  55.7 2.2 %collective-permute-start.15 = (bf16[64,2560]{1,0:T(8,128)(2,1)S(1)}, bf16[64,2560]{1,0:T(8,128)(2,1)S(1)}, u32[]{:S(2)}, u32[]{:S(2)}) collective-permute-start(bf16[64,2560]{1,0:T(8,128)(2,1)S(1)} %get-tuple-element.82), channel_id=1, source_target_pairs={{0,6},{2,4},{4,2},{6,0},{1,7},{3,5},{5,3},{7,1},{8,14},{10,12},{12... | collective-permute-start | bytes 983048 | tf_op jit(solution)/shard_map/ppermute | solution.py:29
  57.9 0.7 collective-permute-done.18.a
  58.6 1.5 %collective-permute-start.16 = (bf16[64,2560]{1,0:T(8,128)(2,1)S(1)}, bf16[64,2560]{1,0:T(8,128)(2,1)S(1)}, u32[]{:S(2)}, u32[]{:S(2)}) collective-permute-start(bf16[64,2560]{1,0:T(8,128)(2,1)S(1)} %get-tuple-element.83), channel_id=1, source_target_pairs={{0,4},{2,6},{4,0},{6,2},{1,5},{3,7},{5,1},{7,3},{8,12},{10,14},{12... | collective-permute-start | bytes 983048 | tf_op jit(solution)/shard_map/ppermute | solution.py:29
  60.1 0.7 collective-permute-done.19.b
  61.2 2.0 %collective-permute-start.21 = (bf16[160,256]{1,0:T(8,128)(2,1)S(1)}, bf16[160,256]{1,0:T(8,128)(2,1)S(1)}, u32[]{:S(2)}, u32[]{:S(2)}) collective-permute-start(bf16[160,256]{1,0:T(8,128)(2,1)S(1)} %get-tuple-element.91), channel_id=1, source_target_pairs={{0,16},{16,0},{32,48},{48,32},{1,17},{17,1},{33,49},{49,33},{2,18}... | collective-permute-start | bytes 245768 | tf_op jit(solution)/shard_map/ppermute | solution.py:29
  63.3 0.5 collective-permute-start.22
  63.8 2.5 %collective-permute-done.14.a = bf16[64,2560]{1,0:T(8,128)(2,1)S(1)} collective-permute-done((bf16[64,2560]{1,0:T(8,128)(2,1)S(1)}, bf16[64,2560]{1,0:T(8,128)(2,1)S(1)}, u32[]{:S(2)}, u32[]{:S(2)}) %collective-permute-start.14) | collective-permute-done | bytes 327712 | tf_op jit(solution)/shard_map/ppermute | solution.py:29
  66.3 1.0 collective-permute-start.23
  67.3 4.3 %collective-permute-done.15.b = bf16[64,2560]{1,0:T(8,128)(2,1)S(1)} collective-permute-done((bf16[64,2560]{1,0:T(8,128)(2,1)S(1)}, bf16[64,2560]{1,0:T(8,128)(2,1)S(1)}, u32[]{:S(2)}, u32[]{:S(2)}) %collective-permute-start.15) | collective-permute-done | bytes 327712 | tf_op jit(solution)/shard_map/ppermute | solution.py:29
  71.6 1.8 %collective-permute-done.16.c = bf16[64,2560]{1,0:T(8,128)(2,1)S(1)} collective-permute-done((bf16[64,2560]{1,0:T(8,128)(2,1)S(1)}, bf16[64,2560]{1,0:T(8,128)(2,1)S(1)}, u32[]{:S(2)}, u32[]{:S(2)}) %collective-permute-start.16) | collective-permute-done | bytes 327712 | tf_op jit(solution)/shard_map/ppermute | solution.py:29
  73.5 1.3 %collective-permute-start.17 = (bf16[32,2560]{1,0:T(8,128)(2,1)S(1)}, bf16[32,2560]{1,0:T(8,128)(2,1)S(1)}, u32[]{:S(2)}, u32[]{:S(2)}) collective-permute-start(bf16[32,2560]{1,0:T(8,128)(2,1)S(1)} %get-tuple-element.85), channel_id=1, source_target_pairs={{0,40},{8,32},{16,56},{24,48},{32,8},{40,0},{48,24},{56,16},{1,41}... | collective-permute-start | bytes 491528 | tf_op jit(solution)/shard_map/ppermute | solution.py:29
  74.9 1.8 %collective-permute-start.24 = (bf16[64,160]{1,0:T(8,128)(2,1)S(1)}, bf16[64,160]{1,0:T(8,128)(2,1)S(1)}, u32[]{:S(2)}, u32[]{:S(2)}) collective-permute-start(bf16[64,160]{1,0:T(8,128)(2,1)S(1)} %convert_element_type.62), channel_id=1, source_target_pairs={{0,4},{2,6},{4,0},{6,2},{1,5},{3,7},{5,1},{7,3},{8,12},{10,14},{12... | collective-permute-start | bytes 61448 | tf_op jit(solution)/shard_map/ppermute | solution.py:29
  76.8 1.0 %collective-permute-start.25 = (bf16[64,160]{1,0:T(8,128)(2,1)S(1)}, bf16[64,160]{1,0:T(8,128)(2,1)S(1)}, u32[]{:S(2)}, u32[]{:S(2)}) collective-permute-start(bf16[64,160]{1,0:T(8,128)(2,1)S(1)} %convert_element_type.62), channel_id=1, source_target_pairs={{0,2},{2,0},{4,6},{6,4},{1,3},{3,1},{5,7},{7,5},{8,10},{10,8},{12,... | collective-permute-start | bytes 61448 | tf_op jit(solution)/shard_map/ppermute | solution.py:29
  77.8 1.4 %collective-permute-start.26 = (bf16[64,160]{1,0:T(8,128)(2,1)S(1)}, bf16[64,160]{1,0:T(8,128)(2,1)S(1)}, u32[]{:S(2)}, u32[]{:S(2)}) collective-permute-start(bf16[64,160]{1,0:T(8,128)(2,1)S(1)} %convert_element_type.62), channel_id=1, source_target_pairs={{0,6},{2,4},{4,2},{6,0},{1,7},{3,5},{5,3},{7,1},{8,14},{10,12},{12... | collective-permute-start | bytes 61448 | tf_op jit(solution)/shard_map/ppermute | solution.py:29
  79.1 1.3 %collective-permute-done.24.a = bf16[64,160]{1,0:T(8,128)(2,1)S(1)} collective-permute-done((bf16[64,160]{1,0:T(8,128)(2,1)S(1)}, bf16[64,160]{1,0:T(8,128)(2,1)S(1)}, u32[]{:S(2)}, u32[]{:S(2)}) %collective-permute-start.24) | collective-permute-done | bytes 20512 | tf_op jit(solution)/shard_map/ppermute | solution.py:29
  80.7 2.2 %collective-permute-done.26.c = bf16[64,160]{1,0:T(8,128)(2,1)S(1)} collective-permute-done((bf16[64,160]{1,0:T(8,128)(2,1)S(1)}, bf16[64,160]{1,0:T(8,128)(2,1)S(1)}, u32[]{:S(2)}, u32[]{:S(2)}) %collective-permute-start.26) | collective-permute-done | bytes 20512 | tf_op jit(solution)/shard_map/ppermute | solution.py:29
  82.9 1.1 %collective-permute-done.17.after.row_got = bf16[32,2560]{1,0:T(8,128)(2,1)S(1)} collective-permute-done((bf16[32,2560]{1,0:T(8,128)(2,1)S(1)}, bf16[32,2560]{1,0:T(8,128)(2,1)S(1)}, u32[]{:S(2)}, u32[]{:S(2)}) %collective-permute-start.17) | collective-permute-done | bytes 163872 | tf_op jit(solution)/shard_map/ppermute | solution.py:29
  84.0 3.8 %collective-permute-start.27 = (bf16[64,160]{1,0:T(8,128)(2,1)S(1)}, bf16[64,160]{1,0:T(8,128)(2,1)S(1)}, u32[]{:S(2)}, u32[]{:S(2)}) collective-permute-start(bf16[64,160]{1,0:T(8,128)(2,1)S(1)} %get-tuple-element.96), channel_id=1, source_target_pairs={{0,8},{8,0},{1,9},{9,1},{2,10},{10,2},{3,11},{11,3},{4,12},{12,4},... | collective-permute-start | bytes 61448 | tf_op jit(solution)/shard_map/ppermute | solution.py:29
  87.7 1.1 %collective-permute-start.29 = (bf16[32,800]{1,0:T(8,128)(2,1)S(1)}, bf16[32,800]{1,0:T(8,128)(2,1)S(1)}, u32[]{:S(2)}, u32[]{:S(2)}) collective-permute-start(bf16[32,800]{1,0:T(8,128)(2,1)S(1)} %get-tuple-element.97.own), channel_id=1, source_target_pairs={{0,64},{64,0},{128,192},{192,128},{1,65},{65,1},{129,193},{193,129... | collective-permute-start | bytes 153608 | tf_op jit(solution)/shard_map/ppermute | solution.py:29
  88.9 2.9 %collective-permute-start.30 = (bf16[32,800]{1,0:T(8,128)(2,1)S(1)}, bf16[32,800]{1,0:T(8,128)(2,1)S(1)}, u32[]{:S(2)}, u32[]{:S(2)}) collective-permute-start(bf16[32,800]{1,0:T(8,128)(2,1)S(1)} %get-tuple-element.97.own), channel_id=1, source_target_pairs={{0,128},{64,192},{128,0},{192,64},{1,129},{65,193},{129,1},{193,65... | collective-permute-start | bytes 153608 | tf_op jit(solution)/shard_map/ppermute | solution.py:29
  91.8 0.7 collective-permute-start.31
  92.6 2.0 %collective-permute-done.30.b = bf16[32,800]{1,0:T(8,128)(2,1)S(1)} collective-permute-done((bf16[32,800]{1,0:T(8,128)(2,1)S(1)}, bf16[32,800]{1,0:T(8,128)(2,1)S(1)}, u32[]{:S(2)}, u32[]{:S(2)}) %collective-permute-start.30) | collective-permute-done | bytes 51232 | tf_op jit(solution)/shard_map/ppermute | solution.py:29
  94.6 2.6 %collective-permute-done.31.c = bf16[32,800]{1,0:T(8,128)(2,1)S(1)} collective-permute-done((bf16[32,800]{1,0:T(8,128)(2,1)S(1)}, bf16[32,800]{1,0:T(8,128)(2,1)S(1)}, u32[]{:S(2)}, u32[]{:S(2)}) %collective-permute-start.31) | collective-permute-done | bytes 51232 | tf_op jit(solution)/shard_map/ppermute | solution.py:29
  97.2 1.1 %finish.1 = (bf16[16,2560]{1,0:T(8,128)(2,1)}, bf16[16,2560]{1,0:T(8,128)(2,1)}, f32[10,32]{1,0:T(8,128)}, f32[10,32]{1,0:T(8,128)}, f32[32,800]{1,0:T(8,128)}, ...) custom-call(s32[1]{0:T(128)} %bitcast.y, ...), custom_call_target="tpu_custom_call" | custom-call | flops 1000 | bytes 1000 | tf_op jit(solution)/shard_map/finish/pallas_call | solution.py:485
  (73 shorter events, 2.2 us)
Async XLA Ops:
  0.6 10.7 %copy-start.8 = (bf16[16,2560]{1,0:T(8,128)(2,1)S(1)}, bf16[16,2560]{1,0:T(8,128)(2,1)}, u32[]{:S(2)}) copy-start(bf16[16,2560]{1,0:T(8,128)(2,1)} %param.14) | copy-start | bytes 245764
  0.7 27.1 %copy-start.3 = (bf16[800,32]{0,1:T(8,128)(2,1)S(1)}, bf16[800,32]{0,1:T(8,128)(2,1)}, u32[]{:S(2)}) copy-start(bf16[800,32]{0,1:T(8,128)(2,1)} %param.22) | copy-start | bytes 153604
  0.7 27.1 %copy-start = (bf16[32,2560]{1,0:T(8,128)(2,1)S(1)}, bf16[32,2560]{1,0:T(8,128)(2,1)}, u32[]{:S(2)}) copy-start(bf16[32,2560]{1,0:T(8,128)(2,1)} %b_down.1) | copy-start | bytes 491524
  0.7 10.7 %copy-start.10 = (f32[800]{0:T(1024)S(1)}, f32[800]{0:T(1024)}, u32[]{:S(2)}) copy-start(f32[800]{0:T(1024)} %param.24) | copy-start | bytes 9604
  0.7 10.7 %copy-start.11 = (f32[800]{0:T(1024)S(1)}, f32[800]{0:T(1024)}, u32[]{:S(2)}) copy-start(f32[800]{0:T(1024)} %param.25) | copy-start | bytes 9604
  0.7 10.7 %copy-start.9 = (f32[2560]{0:T(1024)S(1)}, f32[2560]{0:T(1024)}, u32[]{:S(2)}) copy-start(f32[2560]{0:T(1024)} %param.26) | copy-start | bytes 30724
  0.7 11.9 %copy-start.7 = (bf16[16,2560]{1,0:T(8,128)(2,1)S(1)}, bf16[16,2560]{1,0:T(8,128)(2,1)}, u32[]{:S(2)}) copy-start(bf16[16,2560]{1,0:T(8,128)(2,1)} %param.27) | copy-start | bytes 245764
  0.7 27.0 %copy-start.1 = (bf16[2560,32]{0,1:T(8,128)(2,1)S(1)}, bf16[2560,32]{0,1:T(8,128)(2,1)}, u32[]{:S(2)}) copy-start(bf16[2560,32]{0,1:T(8,128)(2,1)} %param.18) | copy-start | bytes 491524
  0.7 27.0 %copy-start.2 = (bf16[2560,32]{0,1:T(8,128)(2,1)S(1)}, bf16[2560,32]{0,1:T(8,128)(2,1)}, u32[]{:S(2)}) copy-start(bf16[2560,32]{0,1:T(8,128)(2,1)} %param.20) | copy-start | bytes 491524
  0.7 27.0 %copy-start.4 = (bf16[32,800]{1,0:T(8,128)(2,1)S(1)}, bf16[32,800]{1,0:T(8,128)(2,1)}, u32[]{:S(2)}) copy-start(bf16[32,800]{1,0:T(8,128)(2,1)} %b_gate.1) | copy-start | bytes 153604
  0.7 27.0 %copy-start.5 = (bf16[32,800]{1,0:T(8,128)(2,1)S(1)}, bf16[32,800]{1,0:T(8,128)(2,1)}, u32[]{:S(2)}) copy-start(bf16[32,800]{1,0:T(8,128)(2,1)} %b_up.1) | copy-start | bytes 153604
  0.8 9.9 %collective-permute-start = (bf16[16,2560]{1,0:T(8,128)(2,1)}, bf16[16,2560]{1,0:T(8,128)(2,1)S(1)}, u32[]{:S(2)}, u32[]{:S(2)}) collective-permute-start(bf16[16,2560]{1,0:T(8,128)(2,1)} %param.14), channel_id=1, source_target_pairs={{0,40},{8,32},{16,56},{24,48},{32,8},{40,0},{48,24},{56,16},{1,41}... | collective-permute-start | bytes 245768 | tf_op jit(solution)/shard_map/ppermute | solution.py:29
  10.7 0.7 copy-start.6
  11.4 1.2 %collective-permute-start.4 = (f32[1,2560]{1,0:T(1,128)S(1)}, f32[1,2560]{1,0:T(1,128)S(1)}, u32[]{:S(2)}, u32[]{:S(2)}) collective-permute-start(f32[1,2560]{1,0:T(1,128)S(1)} %held_until.1), channel_id=1, source_target_pairs={{0,1},{1,0},{2,3},{3,2},{4,5},{5,4},{6,7},{7,6},{8,9},{9,8},{10,11... | collective-permute-start | bytes 30728 | tf_op jit(solution)/shard_map/ppermute | solution.py:29
  12.6 10.2 %collective-permute-start.5 = (bf16[18,2560]{1,0:T(8,128)(2,1)S(1)}, bf16[18,2560]{1,0:T(8,128)(2,1)S(1)}, u32[]{:S(2)}, u32[]{:S(2)}) collective-permute-start(bf16[18,2560]{1,0:T(8,128)(2,1)S(1)} %pad_maximum_fusion.2), channel_id=1, source_target_pairs={{0,40},{8,32},{16,56},{24,48},{32,8},{40,0},{48,24},{56,16},{1,41}... | collective-permute-start | bytes 276488 | tf_op jit(solution)/shard_map/ppermute | solution.py:29
  15.1 11.6 %collective-permute-start.1 = (bf16[32,2560]{1,0:T(8,128)(2,1)S(1)}, bf16[32,2560]{1,0:T(8,128)(2,1)S(1)}, u32[]{:S(2)}, u32[]{:S(2)}) collective-permute-start(bf16[32,2560]{1,0:T(8,128)(2,1)S(1)} %get-tuple-element.113), channel_id=1, source_target_pairs={{0,2},{2,0},{4,6},{6,4},{1,3},{3,1},{5,7},{7,5},{8,10},{10,8},{12,... | collective-permute-start | bytes 491528 | tf_op jit(solution)/shard_map/ppermute | solution.py:29
  16.7 10.7 %collective-permute-start.2 = (bf16[32,2560]{1,0:T(8,128)(2,1)S(1)}, bf16[32,2560]{1,0:T(8,128)(2,1)S(1)}, u32[]{:S(2)}, u32[]{:S(2)}) collective-permute-start(bf16[32,2560]{1,0:T(8,128)(2,1)S(1)} %get-tuple-element.113), channel_id=1, source_target_pairs={{0,6},{2,4},{4,2},{6,0},{1,7},{3,5},{5,3},{7,1},{8,14},{10,12},{12... | collective-permute-start | bytes 491528 | tf_op jit(solution)/shard_map/ppermute | solution.py:29
  18.8 8.7 %collective-permute-start.3 = (bf16[32,2560]{1,0:T(8,128)(2,1)S(1)}, bf16[32,2560]{1,0:T(8,128)(2,1)S(1)}, u32[]{:S(2)}, u32[]{:S(2)}) collective-permute-start(bf16[32,2560]{1,0:T(8,128)(2,1)S(1)} %get-tuple-element.113), channel_id=1, source_target_pairs={{0,4},{2,6},{4,0},{6,2},{1,5},{3,7},{5,1},{7,3},{8,12},{10,14},{12... | collective-permute-start | bytes 491528 | tf_op jit(solution)/shard_map/ppermute | solution.py:29
  22.9 11.5 %collective-permute-start.6 = (bf16[34,2560]{1,0:T(8,128)(2,1)S(1)}, bf16[34,2560]{1,0:T(8,128)(2,1)S(1)}, u32[]{:S(2)}, u32[]{:S(2)}) collective-permute-start(bf16[34,2560]{1,0:T(8,128)(2,1)S(1)} %pad_maximum_fusion), channel_id=1, source_target_pairs={{0,2},{2,0},{4,6},{6,4},{1,3},{3,1},{5,7},{7,5},{8,10},{10,8},{12,... | collective-permute-start | bytes 522248 | tf_op jit(solution)/shard_map/ppermute | solution.py:29
  24.5 11.9 %collective-permute-start.7 = (bf16[34,2560]{1,0:T(8,128)(2,1)S(1)}, bf16[34,2560]{1,0:T(8,128)(2,1)S(1)}, u32[]{:S(2)}, u32[]{:S(2)}) collective-permute-start(bf16[34,2560]{1,0:T(8,128)(2,1)S(1)} %pad_maximum_fusion), channel_id=1, source_target_pairs={{0,6},{2,4},{4,2},{6,0},{1,7},{3,5},{5,3},{7,1},{8,14},{10,12},{12... | collective-permute-start | bytes 522248 | tf_op jit(solution)/shard_map/ppermute | solution.py:29
  26.6 9.8 %collective-permute-start.8 = (bf16[34,2560]{1,0:T(8,128)(2,1)S(1)}, bf16[34,2560]{1,0:T(8,128)(2,1)S(1)}, u32[]{:S(2)}, u32[]{:S(2)}) collective-permute-start(bf16[34,2560]{1,0:T(8,128)(2,1)S(1)} %pad_maximum_fusion), channel_id=1, source_target_pairs={{0,4},{2,6},{4,0},{6,2},{1,5},{3,7},{5,1},{7,3},{8,12},{10,14},{12... | collective-permute-start | bytes 522248 | tf_op jit(solution)/shard_map/ppermute | solution.py:29
  27.4 9.4 %collective-permute-start.9 = (bf16[128,2560]{1,0:T(8,128)(2,1)S(1)}, bf16[128,2560]{1,0:T(8,128)(2,1)S(1)}, u32[]{:S(2)}, u32[]{:S(2)}) collective-permute-start(bf16[128,2560]{1,0:T(8,128)(2,1)S(1)} %constant_dynamic-update-slice_fusion.2.after.mine), channel_id=1, source_target_pairs={{0,1},{1,0},{2,3},{3,2},{4,5},{5,4},{6,7},{7,6},{8,9},{9,8},{10,11... | collective-permute-start | bytes 1966088 | tf_op jit(solution)/shard_map/ppermute | solution.py:29
  36.5 5.8 %collective-permute-start.11 = (bf16[128,2560]{1,0:T(8,128)(2,1)S(1)}, bf16[128,2560]{1,0:T(8,128)(2,1)S(1)}, u32[]{:S(2)}, u32[]{:S(2)}) collective-permute-start(bf16[128,2560]{1,0:T(8,128)(2,1)S(1)} %join_cot.1.after.cot_mine), channel_id=1, source_target_pairs={{0,1},{1,0},{2,3},{3,2},{4,5},{5,4},{6,7},{7,6},{8,9},{9,8},{10,11... | collective-permute-start | bytes 1966088 | tf_op jit(solution)/shard_map/ppermute | solution.py:29
  46.4 4.0 %collective-permute-start.12 = (bf16[4,64,640]{2,1,0:T(8,128)(2,1)S(1)}, bf16[4,64,640]{2,1,0:T(8,128)(2,1)S(1)}, u32[]{:S(2)}, u32[]{:S(2)}) collective-permute-start(bf16[4,64,640]{2,1,0:T(8,128)(2,1)S(1)} %get-tuple-element.77), channel_id=1, source_target_pairs={{0,1},{1,0},{2,3},{3,2},{4,5},{5,4},{6,7},{7,6},{8,9},{9,8},{10,11... | collective-permute-start | bytes 983048 | tf_op jit(solution)/shard_map/ppermute | solution.py:29
  47.0 8.3 %collective-permute-start.10 = (bf16[128,2560]{1,0:T(8,128)(2,1)S(1)}, bf16[128,2560]{1,0:T(8,128)(2,1)S(1)}, u32[]{:S(2)}, u32[]{:S(2)}) collective-permute-start(bf16[128,2560]{1,0:T(8,128)(2,1)S(1)} %get-tuple-element.66.p_away), channel_id=1, source_target_pairs={{0,1},{1,0},{2,3},{3,2},{4,5},{5,4},{6,7},{7,6},{8,9},{9,8},{10,11... | collective-permute-start | bytes 1966088 | tf_op jit(solution)/shard_map/ppermute | solution.py:29
  50.5 4.8 %collective-permute-start.13 = (bf16[128,2560]{1,0:T(8,128)(2,1)S(1)}, bf16[128,2560]{1,0:T(8,128)(2,1)S(1)}, u32[]{:S(2)}, u32[]{:S(2)}) collective-permute-start(bf16[128,2560]{1,0:T(8,128)(2,1)S(1)} %get-tuple-element.79), channel_id=1, source_target_pairs={{0,1},{1,0},{2,3},{3,2},{4,5},{5,4},{6,7},{7,6},{8,9},{9,8},{10,11... | collective-permute-start | bytes 1966088 | tf_op jit(solution)/shard_map/ppermute | solution.py:29
  51.0 7.5 %collective-permute-start.18 = (bf16[96,640]{1,0:T(8,128)(2,1)S(1)}, bf16[96,640]{1,0:T(8,128)(2,1)S(1)}, u32[]{:S(2)}, u32[]{:S(2)}) collective-permute-start(bf16[96,640]{1,0:T(8,128)(2,1)S(1)} %get-tuple-element.87), channel_id=1, source_target_pairs={{0,128},{64,192},{128,0},{192,64},{1,129},{65,193},{129,1},{193,65... | collective-permute-start | bytes 368648 | tf_op jit(solution)/shard_map/ppermute | solution.py:29
  54.2 6.6 %collective-permute-start.19 = (bf16[96,640]{1,0:T(8,128)(2,1)S(1)}, bf16[96,640]{1,0:T(8,128)(2,1)S(1)}, u32[]{:S(2)}, u32[]{:S(2)}) collective-permute-start(bf16[96,640]{1,0:T(8,128)(2,1)S(1)} %get-tuple-element.88), channel_id=1, source_target_pairs={{0,64},{64,0},{128,192},{192,128},{1,65},{65,1},{129,193},{193,129... | collective-permute-start | bytes 368648 | tf_op jit(solution)/shard_map/ppermute | solution.py:29
  54.9 6.1 %collective-permute-start.20 = (bf16[96,640]{1,0:T(8,128)(2,1)S(1)}, bf16[96,640]{1,0:T(8,128)(2,1)S(1)}, u32[]{:S(2)}, u32[]{:S(2)}) collective-permute-start(bf16[96,640]{1,0:T(8,128)(2,1)S(1)} %get-tuple-element.89), channel_id=1, source_target_pairs={{0,192},{64,128},{128,64},{192,0},{1,193},{65,129},{129,65},{193,1... | collective-permute-start | bytes 368648 | tf_op jit(solution)/shard_map/ppermute | solution.py:29
  55.6 10.7 %collective-permute-start.14 = (bf16[64,2560]{1,0:T(8,128)(2,1)S(1)}, bf16[64,2560]{1,0:T(8,128)(2,1)S(1)}, u32[]{:S(2)}, u32[]{:S(2)}) collective-permute-start(bf16[64,2560]{1,0:T(8,128)(2,1)S(1)} %get-tuple-element.81), channel_id=1, source_target_pairs={{0,2},{2,0},{4,6},{6,4},{1,3},{3,1},{5,7},{7,5},{8,10},{10,8},{12,... | collective-permute-start | bytes 983048 | tf_op jit(solution)/shard_map/ppermute | solution.py:29
  55.7 15.9 %collective-permute-start.15 = (bf16[64,2560]{1,0:T(8,128)(2,1)S(1)}, bf16[64,2560]{1,0:T(8,128)(2,1)S(1)}, u32[]{:S(2)}, u32[]{:S(2)}) collective-permute-start(bf16[64,2560]{1,0:T(8,128)(2,1)S(1)} %get-tuple-element.82), channel_id=1, source_target_pairs={{0,6},{2,4},{4,2},{6,0},{1,7},{3,5},{5,3},{7,1},{8,14},{10,12},{12... | collective-permute-start | bytes 983048 | tf_op jit(solution)/shard_map/ppermute | solution.py:29
  58.6 14.8 %collective-permute-start.16 = (bf16[64,2560]{1,0:T(8,128)(2,1)S(1)}, bf16[64,2560]{1,0:T(8,128)(2,1)S(1)}, u32[]{:S(2)}, u32[]{:S(2)}) collective-permute-start(bf16[64,2560]{1,0:T(8,128)(2,1)S(1)} %get-tuple-element.83), channel_id=1, source_target_pairs={{0,4},{2,6},{4,0},{6,2},{1,5},{3,7},{5,1},{7,3},{8,12},{10,14},{12... | collective-permute-start | bytes 983048 | tf_op jit(solution)/shard_map/ppermute | solution.py:29
  61.2 13.6 %collective-permute-start.21 = (bf16[160,256]{1,0:T(8,128)(2,1)S(1)}, bf16[160,256]{1,0:T(8,128)(2,1)S(1)}, u32[]{:S(2)}, u32[]{:S(2)}) collective-permute-start(bf16[160,256]{1,0:T(8,128)(2,1)S(1)} %get-tuple-element.91), channel_id=1, source_target_pairs={{0,16},{16,0},{32,48},{48,32},{1,17},{17,1},{33,49},{49,33},{2,18}... | collective-permute-start | bytes 245768 | tf_op jit(solution)/shard_map/ppermute | solution.py:29
  63.3 11.6 %collective-permute-start.22 = (bf16[160,256]{1,0:T(8,128)(2,1)S(1)}, bf16[160,256]{1,0:T(8,128)(2,1)S(1)}, u32[]{:S(2)}, u32[]{:S(2)}) collective-permute-start(bf16[160,256]{1,0:T(8,128)(2,1)S(1)} %get-tuple-element.92), channel_id=1, source_target_pairs={{0,32},{16,48},{32,0},{48,16},{1,33},{17,49},{33,1},{49,17},{2,34}... | collective-permute-start | bytes 245768 | tf_op jit(solution)/shard_map/ppermute | solution.py:29
  66.3 8.5 %collective-permute-start.23 = (bf16[160,256]{1,0:T(8,128)(2,1)S(1)}, bf16[160,256]{1,0:T(8,128)(2,1)S(1)}, u32[]{:S(2)}, u32[]{:S(2)}) collective-permute-start(bf16[160,256]{1,0:T(8,128)(2,1)S(1)} %get-tuple-element.93), channel_id=1, source_target_pairs={{0,48},{16,32},{32,16},{48,0},{1,49},{17,33},{33,17},{49,1},{2,50}... | collective-permute-start | bytes 245768 | tf_op jit(solution)/shard_map/ppermute | solution.py:29
  73.5 10.4 %collective-permute-start.17 = (bf16[32,2560]{1,0:T(8,128)(2,1)S(1)}, bf16[32,2560]{1,0:T(8,128)(2,1)S(1)}, u32[]{:S(2)}, u32[]{:S(2)}) collective-permute-start(bf16[32,2560]{1,0:T(8,128)(2,1)S(1)} %get-tuple-element.85), channel_id=1, source_target_pairs={{0,40},{8,32},{16,56},{24,48},{32,8},{40,0},{48,24},{56,16},{1,41}... | collective-permute-start | bytes 491528 | tf_op jit(solution)/shard_map/ppermute | solution.py:29
  74.9 5.5 %collective-permute-start.24 = (bf16[64,160]{1,0:T(8,128)(2,1)S(1)}, bf16[64,160]{1,0:T(8,128)(2,1)S(1)}, u32[]{:S(2)}, u32[]{:S(2)}) collective-permute-start(bf16[64,160]{1,0:T(8,128)(2,1)S(1)} %convert_element_type.62), channel_id=1, source_target_pairs={{0,4},{2,6},{4,0},{6,2},{1,5},{3,7},{5,1},{7,3},{8,12},{10,14},{12... | collective-permute-start | bytes 61448 | tf_op jit(solution)/shard_map/ppermute | solution.py:29
  76.8 3.9 %collective-permute-start.25 = (bf16[64,160]{1,0:T(8,128)(2,1)S(1)}, bf16[64,160]{1,0:T(8,128)(2,1)S(1)}, u32[]{:S(2)}, u32[]{:S(2)}) collective-permute-start(bf16[64,160]{1,0:T(8,128)(2,1)S(1)} %convert_element_type.62), channel_id=1, source_target_pairs={{0,2},{2,0},{4,6},{6,4},{1,3},{3,1},{5,7},{7,5},{8,10},{10,8},{12,... | collective-permute-start | bytes 61448 | tf_op jit(solution)/shard_map/ppermute | solution.py:29
  77.8 5.1 %collective-permute-start.26 = (bf16[64,160]{1,0:T(8,128)(2,1)S(1)}, bf16[64,160]{1,0:T(8,128)(2,1)S(1)}, u32[]{:S(2)}, u32[]{:S(2)}) collective-permute-start(bf16[64,160]{1,0:T(8,128)(2,1)S(1)} %convert_element_type.62), channel_id=1, source_target_pairs={{0,6},{2,4},{4,2},{6,0},{1,7},{3,5},{5,3},{7,1},{8,14},{10,12},{12... | collective-permute-start | bytes 61448 | tf_op jit(solution)/shard_map/ppermute | solution.py:29
  84.0 8.5 %collective-permute-start.27 = (bf16[64,160]{1,0:T(8,128)(2,1)S(1)}, bf16[64,160]{1,0:T(8,128)(2,1)S(1)}, u32[]{:S(2)}, u32[]{:S(2)}) collective-permute-start(bf16[64,160]{1,0:T(8,128)(2,1)S(1)} %get-tuple-element.96), channel_id=1, source_target_pairs={{0,8},{8,0},{1,9},{9,1},{2,10},{10,2},{3,11},{11,3},{4,12},{12,4},... | collective-permute-start | bytes 61448 | tf_op jit(solution)/shard_map/ppermute | solution.py:29
  87.7 4.8 %collective-permute-start.29 = (bf16[32,800]{1,0:T(8,128)(2,1)S(1)}, bf16[32,800]{1,0:T(8,128)(2,1)S(1)}, u32[]{:S(2)}, u32[]{:S(2)}) collective-permute-start(bf16[32,800]{1,0:T(8,128)(2,1)S(1)} %get-tuple-element.97.own), channel_id=1, source_target_pairs={{0,64},{64,0},{128,192},{192,128},{1,65},{65,1},{129,193},{193,129... | collective-permute-start | bytes 153608 | tf_op jit(solution)/shard_map/ppermute | solution.py:29
  88.9 5.7 %collective-permute-start.30 = (bf16[32,800]{1,0:T(8,128)(2,1)S(1)}, bf16[32,800]{1,0:T(8,128)(2,1)S(1)}, u32[]{:S(2)}, u32[]{:S(2)}) collective-permute-start(bf16[32,800]{1,0:T(8,128)(2,1)S(1)} %get-tuple-element.97.own), channel_id=1, source_target_pairs={{0,128},{64,192},{128,0},{192,64},{1,129},{65,193},{129,1},{193,65... | collective-permute-start | bytes 153608 | tf_op jit(solution)/shard_map/ppermute | solution.py:29
  91.8 5.4 %collective-permute-start.31 = (bf16[32,800]{1,0:T(8,128)(2,1)S(1)}, bf16[32,800]{1,0:T(8,128)(2,1)S(1)}, u32[]{:S(2)}, u32[]{:S(2)}) collective-permute-start(bf16[32,800]{1,0:T(8,128)(2,1)S(1)} %get-tuple-element.97.own), channel_id=1, source_target_pairs={{0,192},{64,128},{128,64},{192,0},{1,193},{65,129},{129,65},{193,1... | collective-permute-start | bytes 153608 | tf_op jit(solution)/shard_map/ppermute | solution.py:29
  92.5 4.7 %collective-permute-start.28 = (f32[64,160]{1,0:T(8,128)S(1)}, f32[64,160]{1,0:T(8,128)S(1)}, u32[]{:S(2)}, u32[]{:S(2)}) collective-permute-start(f32[64,160]{1,0:T(8,128)S(1)} %convert_add_fusion.shared), channel_id=1, source_target_pairs={{0,1},{1,0},{2,3},{3,2},{4,5},{5,4},{6,7},{7,6},{8,9},{9,8},{10,11... | collective-permute-start | bytes 122888 | tf_op jit(solution)/shard_map/ppermute | solution.py:29
